TPU v7x, 32 devices: a whole 2x2x4 slice. The times are simulated.
32 devices in a mesh: gx: 8 (over z, y), gz: 4 (over x, core).
Axes of the slice: x: 2, y: 2, z: 4, core: 2. Of those that a mesh axis runs over, the one named last changes fastest.
Arguments:
- thermal_undercool: float32 [16, 384, 512], P(None, 'gx', 'gz'), may hold values from -1 to 1
- mixture_alloying: float32 [16, 384, 512], P(None, 'gx', 'gz'), may hold values from 0.5 to 1.5
- fluid_fraction: float32 [16, 384, 512], P(None, 'gx', 'gz'), may hold values from 0.05 to 0.95
- kozeny_factor: float32 [16, 384, 512], P(None, 'gx', 'gz'), may hold values from 0.5 to 2
- state_marker: int32 [16, 384, 512], P(None, 'gx', 'gz'), may hold values from 0 to 2
Outputs:
- pressure: float32 [16, 384, 512], P(None, 'gx', 'gz')
- solute_out: float32 [16, 384, 512], P(None, 'gx', 'gz')
Inputs may be any that keep to these rules, and one draw needn't show every extreme that they name: `state_marker`: 0 marks a mushy cell, 1 a liquid one, 2 a solid one.
All inputs are finite; a program needn't handle non-finite values.
Results may differ from a plain program's by a relative error of at most 0.0003.
Values sent between devices are 32-bit elements; how exact they have to be, the bound alone decides.
A program may use at most 64 MiB of HBM per device.

v0:
```python
import functools

import jax
import jax.numpy as jnp
from jax import lax
from jax.experimental import pallas as pl
from jax.experimental.pallas import tpu as pltpu
from jax.sharding import PartitionSpec as P

STEPS = 4
SWEEPS = 3
W = SWEEPS + 1
SOLUTE_RATE = 0.5
MESH = pl.DeviceIdType.MESH
UNROLL = 4

LO = 8


def kernel(nx, nz, *refs):
    it = iter(refs)
    hbm = [next(it) for _ in range(5)]
    p_out, c_out = [next(it) for _ in range(2)]
    t_in, c_in, f_in, k_in, m_in = staged = [next(it) for _ in range(5)]
    perm, temp, ca, cb, pa, pb = [next(it) for _ in range(6)]
    axp, axm, ayp, aym, azp, azm, srcn = [next(it) for _ in range(7)]
    cxp, cyp, czp, czm, rl, bb, ld, lu = [next(it) for _ in range(8)]
    hf = next(it)
    off, totp, hl, pf, hx, hxt = [next(it) for _ in range(6)]
    xs, xr, zs, zr, es, er, ts, tr = [next(it) for _ in range(8)]
    sxs, sxr, szs, szr, ses, ser = [next(it) for _ in range(6)]
    send_sem, recv_sem, st_send, st_recv, in_sem = [next(it) for _ in range(5)]

    ny, n, lanes = t_in.shape
    wide = n + 2 * W
    hi_row = LO + wide
    mid = LO + W
    gravity = 4.0 / (nz * lanes)
    half = 0.5 * gravity
    ix, iz = lax.axis_index("gx"), lax.axis_index("gz")
    f32, bf16 = jnp.float32, jnp.bfloat16

    CONC, PERM, TEMP, SRC, PH, BH, AXP, AXM, AYP, AYM, AZP, AZM, SRCN, RHO = range(14)

    def inside(dx, dz):
        return (ix + dx >= 0) & (ix + dx < nx) & (iz + dz >= 0) & (iz + dz < nz)

    partners = [(dx, dz) for dz in range(-1, nz) for dx in (-1, 0, 1) if (dx, dz) != (0, 0)]

    def step_copies(s, totals):
        plan = []
        for dx, dz in partners:
            a, b = (1, 0) if dx > 0 else (0, 1)
            if dz == 0:
                plan.append((dx, dz, xs.at[s, a], xr.at[s, b]))
            elif dz in (-1, 1) and dx == 0:
                plan.append((dx, dz, zs.at[s], zr.at[s, 0 if dz > 0 else 1]))
            elif dz in (-1, 1):
                plan.append((dx, dz, es.at[s, a], er.at[s, b, 0 if dz > 0 else 1]))
            if dz > 0:
                plan.append((dx, dz, ts.at[s], tr.at[s, 1 - dx, dz - 1]))
        return [(dx, dz, pltpu.make_async_remote_copy(
            src_ref=src, dst_ref=dst, send_sem=send_sem.at[s, m], recv_sem=recv_sem.at[s, m],
            device_id={"gx": ix + dx, "gz": iz + dz}, device_id_type=MESH))
            for m, (dx, dz, src, dst) in enumerate(plan) if (dst.shape == (8, lanes)) == totals]

    def static_copies():
        out = []
        for dx, dz in partners:
            if dz > 1:
                continue
            a, b = (1, 0) if dx > 0 else (0, 1)
            if dz == 0:
                src, dst = sxs.at[a], sxr.at[b]
            elif dx == 0:
                src, dst = szs, szr.at[0 if dz > 0 else 1]
            else:
                src, dst = ses.at[a], ser.at[b, 0 if dz > 0 else 1]
            m = len(out)
            out.append((dx, dz, pltpu.make_async_remote_copy(
                src_ref=src, dst_ref=dst, send_sem=st_send.at[m], recv_sem=st_recv.at[m],
                device_id={"gx": ix + dx, "gz": iz + dz}, device_id_type=MESH)))
        return out

    def start(copies):
        for dx, dz, c in copies:
            pl.when(inside(dx, dz))(c.start)

    def arrive(copies):
        for dx, dz, c in copies:
            pl.when(inside(-dx, -dz))(c.wait_recv)

    def sent(copies):
        for dx, dz, c in copies:
            pl.when(inside(dx, dz))(c.wait_send)

    loads = [pltpu.make_async_copy(a, b, in_sem.at[i]) for i, (a, b) in enumerate(zip(hbm, staged))]
    for load in loads:
        load.start()

    for ref in (xr, zr, er, tr, sxr, szr, ser):
        ref[...] = jnp.zeros_like(ref)
    barrier = pltpu.get_barrier_semaphore()
    count = 0
    for dx, dz in partners:
        @pl.when(inside(-dx, -dz))
        def _(dx=dx, dz=dz):
            pl.semaphore_signal(barrier, inc=1, device_id={"gx": ix - dx, "gz": iz - dz}, device_id_type=MESH)
        count = count + inside(dx, dz).astype(jnp.int32)

    def yloop(body, init):
        def group(g, carry):
            for u in range(UNROLL):
                carry = body(g * UNROLL + u, carry)
            return carry
        return lax.fori_loop(0, ny // UNROLL, group, init)

    lane_n = lax.broadcasted_iota(jnp.int32, (n, lanes), 1)
    lane_w = lax.broadcasted_iota(jnp.int32, (wide, lanes), 1)
    per = lanes // ny

    def lane(rows):
        return lane_n if rows == n else lane_w

    def fold(acc, value, y, roll=True):
        moved = pltpu.roll(value, y * per + W, 1) if roll else value
        return jnp.where(lane(value.shape[0]) // per == y, moved, acc)

    def z_near(value, packed, y):
        e = pltpu.roll(packed, lanes - W - y * per, 1)
        ln = lane(value.shape[0])
        up = pltpu.roll(jnp.where(ln == lanes - 1, e, value), 1, 1)
        down = pltpu.roll(jnp.where(ln == 0, e, value), lanes - 1, 1)
        return down, up

    k_w = lane_w % per

    def z_near_packed(packed, own):
        up = pltpu.roll(jnp.where(k_w == W - 1, own, packed), 1, 1)
        down = pltpu.roll(jnp.where(k_w == W, own, packed), lanes - 1, 1)
        return down, up

    def y_near_packed(packed):
        return pltpu.roll(packed, lanes - per, 1), pltpu.roll(packed, per, 1)

    def split(value):
        high = value.astype(bf16)
        low = (value - high.astype(f32)).astype(bf16)
        return jnp.concatenate([high, low], axis=1)

    def split_dot(value, weights):
        return jnp.dot(split(value), weights, preferred_element_type=f32)

    r2 = lax.broadcasted_iota(jnp.int32, (2 * lanes, lanes), 0) % lanes
    c2 = lax.broadcasted_iota(jnp.int32, (2 * lanes, lanes), 1)
    ones = jnp.ones((2 * lanes, lanes), bf16)
    before = jnp.where(r2 < c2, 1.0, jnp.where(r2 == c2, 0.5, 0.0)).astype(bf16)
    both = jnp.concatenate([before, ones], axis=1)
    kr, kc = r2 % per, c2 % per
    same = (r2 // per) == (c2 // per)
    after_w = jnp.where(kr == kc, 0.5, jnp.where((kr >= W) & (kr < kc), 1.0, 0.0))
    before_w = jnp.where(kr == kc, -0.5, jnp.where((kr < W) & (kr > kc), -1.0, 0.0))
    spread_w = jnp.where(same, 1.0, 0.0).astype(bf16)
    packed_sum = jnp.where(same, jnp.where(kc >= W, after_w, before_w), 0.0).astype(bf16)

    zslab = jnp.zeros(perm.shape[1:], f32)
    for ref in (perm, ca, cb, pa, pb):
        ref[0] = zslab
        ref[ny + 1] = zslab
    zrows = jnp.zeros((LO, lanes), f32)

    def clear(y, carry):
        for ref in (perm, pa, pb, ca, cb):
            ref[y + 1, 0:LO, :] = zrows
            ref[y + 1, hi_row:hi_row + LO, :] = zrows
        return carry
    yloop(clear, 0)
    cyp[0] = zslab
    cxp[:, 0:LO, :] = jnp.zeros((ny, LO, lanes), f32)
    hf[...] = jnp.zeros_like(hf)

    for load in loads:
        load.wait()
    zn = jnp.zeros((n, lanes), f32)
    center = pl.ds(mid, n)
    window = pl.ds(LO, wide)

    def own_fields(y, carry):
        zp, zt, zsr, zc = carry
        mark, t, c = m_in[y], t_in[y], c_in[y]
        liq = jnp.where(mark == 1, 1.0, jnp.where(mark == 2, 0.0, f_in[y]))
        solid = 1.0 - liq
        pm = k_in[y] * (liq * liq * liq / (solid * solid + 0.25) + 0.02)
        sr = 2.0 * liq * solid * t
        perm[y + 1, center, :] = pm
        temp[y, center, :] = t
        srcn[y, center, :] = sr
        ca[y + 1, center, :] = c
        rl[y] = SOLUTE_RATE / (liq + 0.1)
        for f, v in enumerate((pm, t, sr)):
            sxs[0, f, y] = v[0:W]
            sxs[1, f, y] = v[n - W:n]
        xs[0, 0, y] = c[0:W]
        xs[0, 1, y] = c[n - W:n]
        hl[y] = split(1.0 + 0.2 * c - 0.3 * t)
        return fold(zp, pm, y), fold(zt, t, y), fold(zsr, sr, y), fold(zc, c, y)

    lane_8 = lax.broadcasted_iota(jnp.int32, (8, lanes), 1)

    def post(s, zc):
        zs[s] = zc
        es[s, 0] = zc[0:W]
        es[s, 1] = zc[n - W:n]
        start(step_copies(s, False))
        sums = jnp.dot(hl[...].reshape(ny * n, 2 * lanes), both, preferred_element_type=f32)
        pf[:, center, :] = sums[:, 0:lanes].reshape(ny, n, lanes)
        totals = sums[:, lanes:2 * lanes].reshape(ny, n, lanes)
        tot = zn
        for y in range(ny):
            tot = jnp.where(lane_n // per == y, totals[y], tot)
        totp[center, :] = tot
        packed = jnp.zeros((8, lanes), f32)
        for j in range(n // 8):
            packed = jnp.where(lane_8 % per == j, tot[8 * j:8 * j + 8], packed)
        ts[s] = packed
        start(step_copies(s, True))

    zp, zt, zsr, zc = yloop(own_fields, (zn,) * 4)
    for f, v in enumerate((zp, zt, zsr)):
        szs[f] = v
        ses[0, f] = v[0:W]
        ses[1, f] = v[n - W:n]
    pl.semaphore_wait(barrier, count)
    start(static_copies())
    post(0, zc)

    top, bottom = pl.ds(LO, W), pl.ds(mid + n, W)
    k_n = lane_n % per
    k_e = lax.broadcasted_iota(jnp.int32, (W, lanes), 1) % per

    arrive(static_copies())
    for f, h in enumerate((PERM, TEMP, SRC)):
        hf[h, center, :] = jnp.where(k_n < W, szr[0, f], szr[1, f])
        hf[h, top, :] = jnp.where(k_e < W, ser[0, 0, f], ser[0, 1, f])
        hf[h, bottom, :] = jnp.where(k_e < W, ser[1, 0, f], ser[1, 1, f])

    def spread(y, carry):
        for f, (ref, o) in enumerate(((perm, 1), (temp, 0), (srcn, 0))):
            ref[y + o, top, :] = sxr[0, f, y]
            ref[y + o, bottom, :] = sxr[1, f, y]
        return carry
    yloop(spread, 0)

    up_rows, down_rows = pl.ds(LO + 1, wide), pl.ds(LO - 1, wide)

    def diagonal_of(pm, near):
        c = [0.5 * (pm + other) for other in near]
        total = c[0] + c[1] + c[2] + c[3] + c[4] + c[5]
        inv = jnp.where(pm > 0.0, 1.0 / jnp.where(pm > 0.0, total, 1.0), 0.0)
        return c, inv

    def coefficients(y, acc):
        pm = perm[y + 1, window, :]
        dz, uz = z_near(pm, hf[PERM, window, :], y)
        c, inv = diagonal_of(pm, [perm[y + 1, up_rows, :], perm[y + 1, down_rows, :],
                                  perm[y + 2, window, :], perm[y, window, :], dz, uz])
        cxp[y, window, :] = c[0]
        cyp[y + 1, window, :] = c[2]

        @pl.when(y == 0)
        def _():
            cyp[0, window, :] = c[3]
        czp[y, window, :] = c[4]
        czm[y, window, :] = c[5]
        for ref, v in zip((axp, axm, ayp, aym, azp, azm), c):
            ref[y] = v * inv
        srcn[y, window, :] = srcn[y, window, :] * inv
        return fold(acc, pm, y)

    zw = jnp.zeros((wide, lanes), f32)
    own = yloop(coefficients, zw)
    pm = hf[PERM, window, :]
    yp, ym = y_near_packed(pm)
    first, last = lane_w < per, lane_w >= lanes - per
    yp, ym = jnp.where(last, 0.0, yp), jnp.where(first, 0.0, ym)
    dz, uz = z_near_packed(pm, own)
    c, inv = diagonal_of(pm, [hf[PERM, up_rows, :], hf[PERM, down_rows, :], yp, ym, dz, uz])
    c[2], c[3] = jnp.where(last, 0.0, c[2]), jnp.where(first, 0.0, c[3])
    for h, v in zip((AXP, AXM, AYP, AYM, AZP, AZM, SRCN), c + [hf[SRC, window, :]]):
        hf[h, window, :] = v * inv

    hx[:, 0:W, :] = sxr[0, 1]
    hx[:, W:2 * W, :] = sxr[1, 1]
    hxt[...] = hx[...]

    conc, conc_next = ca, cb
    for s in range(STEPS):
        arrive(step_copies(s, False))
        hf[CONC, center, :] = jnp.where(k_n < W, zr[s, 0], zr[s, 1])
        hf[CONC, top, :] = jnp.where(k_e < W, er[s, 0, 0], er[s, 0, 1])
        hf[CONC, bottom, :] = jnp.where(k_e < W, er[s, 1, 0], er[s, 1, 1])
        hx[:, 0:W, :] = xr[s, 0]
        hx[:, W:2 * W, :] = xr[s, 1]
        strips = split_dot(1.0 + 0.2 * hx[...].reshape(ny * 2 * W, lanes) - 0.3 * hxt[...].reshape(ny * 2 * W, lanes), both)
        heads = strips[:, 0:lanes].reshape(ny, 2 * W, lanes)
        pf[:, top, :] = heads[:, 0:W]
        pf[:, bottom, :] = heads[:, W:2 * W]
        tails = strips[:, lanes:2 * lanes].reshape(ny, 2 * W, lanes)
        tot = jnp.zeros((2 * W, lanes), f32)
        for y in range(ny):
            tot = jnp.where(lane_8 // per == y, tails[y], tot)
        totp[top, :] = tot[0:W]
        totp[bottom, :] = tot[W:2 * W]
        hpm = hf[PERM, window, :]
        hrho = jnp.where(hpm > 0.0, 1.0 + 0.2 * hf[CONC, window, :] - 0.3 * hf[TEMP, window, :], 0.0)
        hf[RHO, window, :] = hrho

        def head(y, acc, conc=conc, s=s):
            conc[y + 1, top, :] = xr[s, 0, y]
            conc[y + 1, bottom, :] = xr[s, 1, y]
            real = perm[y + 1, window, :] > 0.0
            rho = jnp.where(real, 1.0 + 0.2 * conc[y + 1, window, :] - 0.3 * temp[y, window, :], 0.0)
            pa[y + 1, window, :] = jnp.where(real, gravity * pf[y, window, :], 0.0)
            dz, uz = z_near(rho, hf[RHO, window, :], y)
            down, up = half * (rho + dz), half * (rho + uz)
            ld[y, window, :] = down
            lu[y, window, :] = up
            bb[y] = srcn[y, window, :] - azp[y] * down + azm[y] * up
            return fold(acc, rho, y)

        own = yloop(head, zw)
        arrive(step_copies(s, True))
        total = [tr[s, side, 0] for side in range(3)]
        for d in range(1, nz - 1):
            total = [total[side] + tr[s, side, d] for side in range(3)]
        for j in range(n // 8):
            off[pl.ds(mid + 8 * j, 8), :] = jnp.where(lane_8 % per == j, total[1], 0.0)
        off[top, :] = jnp.where(lane_8 % per == n // 8 - 1, total[0], 0.0)[8 - W:8]
        off[bottom, :] = jnp.where(lane_8 % per == 0, total[2], 0.0)[0:W]
        off[window, :] = split_dot(off[window, :], spread_w)

        def lower(y, carry):
            real = perm[y + 1, window, :] > 0.0
            above = pltpu.roll(off[window, :], lanes - W - y * per, 1)[:, 0:1]
            pa[y + 1, window, :] = pa[y + 1, window, :] + jnp.where(real, gravity * above, 0.0)
            return carry
        yloop(lower, 0)
        above = off[window, :]
        above = jnp.where(k_w >= W, above + totp[window, :], above)
        hf[PH, window, :] = jnp.where(hpm > 0.0, gravity * (above + split_dot(hrho, packed_sum)), 0.0)
        dz, uz = z_near_packed(hrho, own)
        hf[BH, window, :] = hf[SRCN, window, :] - half * (
            hf[AZP, window, :] * (hrho + dz) - hf[AZM, window, :] * (hrho + uz))

        old, new = pa, pb
        for sweep in range(SWEEPS):
            def relax(y, acc, old=old, new=new):
                p = old[y + 1, window, :]
                dz, uz = z_near(p, hf[PH, window, :], y)
                v = bb[y] + axp[y] * old[y + 1, up_rows, :] + axm[y] * old[y + 1, down_rows, :]
                v = v + (ayp[y] * old[y + 2, window, :] + aym[y] * old[y, window, :])
                v = v + (azp[y] * dz + azm[y] * uz)
                new[y + 1, window, :] = v
                return fold(acc, p, y)

            own = yloop(relax, zw)
            p = hf[PH, window, :]
            dz, uz = z_near_packed(p, own)
            yp, ym = y_near_packed(p)
            v = hf[BH, window, :] + hf[AXP, window, :] * hf[PH, up_rows, :] + hf[AXM, window, :] * hf[PH, down_rows, :]
            v = v + hf[AYP, window, :] * yp + hf[AYM, window, :] * ym
            v = v + hf[AZP, window, :] * dz + hf[AZM, window, :] * uz
            hf[PH, window, :] = v
            old, new = new, old

        final = s == STEPS - 1
        up_c, down_c = pl.ds(mid + 1, n), pl.ds(mid - 1, n)

        def transport(y, zc, old=old, conc=conc, conc_next=conc_next, s=s, final=final):
            p, c = old[y + 1, center, :], conc[y + 1, center, :]
            pdz, puz = z_near(p, hf[PH, center, :], y)
            cdz, cuz = z_near(c, hf[CONC, center, :], y)

            def carried(flow, near):
                return flow * jnp.where(flow > 0.0, c, near)

            change = carried(cxp[y, center, :] * (p - old[y + 1, up_c, :]), conc[y + 1, up_c, :])
            change = change + carried(cxp[y, down_c, :] * (p - old[y + 1, down_c, :]), conc[y + 1, down_c, :])
            change = change + carried(cyp[y + 1, center, :] * (p - old[y + 2, center, :]), conc[y + 2, center, :])
            change = change + carried(cyp[y, center, :] * (p - old[y, center, :]), conc[y, center, :])
            change = change + carried(czp[y, center, :] * (p - pdz + ld[y, center, :]), cdz)
            change = change + carried(czm[y, center, :] * (p - puz - lu[y, center, :]), cuz)
            fresh = c - rl[y] * change
            if final:
                p_out[y] = p
                c_out[y] = fresh
                return zc
            conc_next[y + 1, center, :] = fresh
            xs[s + 1, 0, y] = fresh[0:W]
            xs[s + 1, 1, y] = fresh[n - W:n]
            hl[y] = split(1.0 + 0.2 * fresh - 0.3 * t_in[y])
            return fold(zc, fresh, y)

        if final:
            yloop(transport, 0)
        else:
            post(s + 1, yloop(transport, zn))
        conc, conc_next = conc_next, conc

    sent(static_copies())
    for s in range(STEPS):
        sent(step_copies(s, False))
        sent(step_copies(s, True))


def on_device(nx, nz, *args):
    ny, n, lanes = args[0].shape
    wide = n + 2 * W
    rows = wide + 2 * LO
    copies = 2 + 6 + 3 * (nz - 1)

    def vmem(*shape):
        return pltpu.VMEM(shape, jnp.float32)

    padded, layered = (ny + 2, rows, lanes), (ny, rows, lanes)
    scratch = [pltpu.VMEM((ny, n, lanes), a.dtype) for a in args]
    scratch += [vmem(*padded), vmem(*layered)] + [vmem(*padded)] * 4
    scratch += [vmem(ny, wide, lanes)] * 6 + [vmem(*layered)]
    scratch += [vmem(*layered), vmem(ny + 1, rows, lanes), vmem(*layered), vmem(*layered),
                vmem(ny, n, lanes), vmem(ny, wide, lanes), vmem(*layered), vmem(*layered)]
    scratch += [vmem(14, rows, lanes), vmem(rows, lanes), vmem(rows, lanes)]
    scratch += [pltpu.VMEM((ny, n, 2 * lanes), jnp.bfloat16), vmem(*layered)] + [vmem(ny, 2 * W, lanes)] * 2
    scratch += [vmem(STEPS, 2, ny, W, lanes)] * 2
    scratch += [vmem(STEPS, n, lanes), vmem(STEPS, 2, n, lanes)]
    scratch += [vmem(STEPS, 2, W, lanes), vmem(STEPS, 2, 2, W, lanes)]
    scratch += [vmem(STEPS, 8, lanes), vmem(STEPS, 3, nz - 1, 8, lanes)]
    scratch += [vmem(2, 3, ny, W, lanes)] * 2
    scratch += [vmem(3, n, lanes), vmem(2, 3, n, lanes), vmem(2, 3, W, lanes), vmem(2, 2, 3, W, lanes)]
    scratch += [pltpu.SemaphoreType.DMA((STEPS, copies))] * 2 + [pltpu.SemaphoreType.DMA((8,))] * 2
    scratch += [pltpu.SemaphoreType.DMA((5,))]
    return tuple(pl.pallas_call(
        functools.partial(kernel, nx, nz),
        out_shape=[jax.ShapeDtypeStruct((ny, n, lanes), jnp.float32)] * 2,
        in_specs=[pl.BlockSpec(memory_space=pltpu.HBM)] * 5,
        out_specs=[pl.BlockSpec(memory_space=pltpu.VMEM)] * 2,
        scratch_shapes=scratch,
        compiler_params=pltpu.CompilerParams(
            collective_id=0, has_side_effects=True, vmem_limit_bytes=63 * 1024 * 1024),
    )(*args))


def solution(mesh):
    placed = P(None, "gx", "gz")
    return jax.shard_map(
        functools.partial(on_device, mesh.shape["gx"], mesh.shape["gz"]),
        mesh=mesh,
        in_specs=(placed,) * 5,
        out_specs=(placed, placed),
        check_vma=False,
    )
```

profile of v0, /device:TPU:9, one launch (start us, length us, event | category | flops | bytes accessed | tf_op | source)
XLA Modules:
  0.0 57.4 jit_solution(6562821058915152434)
XLA Ops:
  0.6 54.1 %shard_map.68 = (f32[16,48,128]{2,1,0:T(8,128)}, f32[16,48,128]{2,1,0:T(8,128)}) custom-call(f32[16,48,128]{2,1,0:T(8,128)} %refs_0_.1, f32[16,48,128]{2,1,0:T(8,128)} %refs_1_.1, f32[16,48,128]{2,1,0:T(8,128)} %refs_2_.1, f32[16,48,128]{2,1,0:T(8,128)} %refs_3_.1, s32[16,48,128]{2,1,0:T(8,128)} %refs_4_.1), custom_call_target="tpu_custom_call" | custom-call | tf_op jit(solution)/shard_map/pallas_call | solution.py:441
  54.8 0.0 copy-start
  54.8 1.8 %copy.9 = f32[16,48,128]{2,1,0:T(8,128)} copy(f32[16,48,128]{2,1,0:T(8,128)} %get-tuple-element.4) | data formatting | bytes 786432
  56.6 0.0 copy-done
  56.6 0.7 %copy.10 = f32[16,48,128]{2,1,0:T(8,128)} copy(f32[16,48,128]{2,1,0:T(8,128)S(1)} %copy-done) | data formatting | bytes 786432
Async XLA Ops:
  54.8 1.8 %copy-start = (f32[16,48,128]{2,1,0:T(8,128)S(1)}, f32[16,48,128]{2,1,0:T(8,128)}, u32[]{:S(2)}) copy-start(f32[16,48,128]{2,1,0:T(8,128)} %get-tuple-element.5) | copy-start | bytes 1179652
where the time goes:
time: 58 us; the launch traced here: 57.4 us
  Pallas kernels  54.1 us (93%)
  local copies, waits for them, and re-layouts  2.57 us (4%)
  between operations  0.65 us (1%)
    pallas_call x1, Pallas kernels, on_device(): pl.pallas_call(functools.partial(kernel, nx, nz), out_shape=[jax.ShapeDty...  54.1 us
    unnamed x4, local copies, waits for them, and re-layouts  2.57 us

commit v1 on v0

v1 whole, which is shorter than its diff:
```python
import functools

import jax
import jax.numpy as jnp
from jax import lax
from jax.experimental import pallas as pl
from jax.experimental.pallas import tpu as pltpu
from jax.sharding import PartitionSpec as P

STEPS = 4
SWEEPS = 3
W = SWEEPS + 1
SOLUTE_RATE = 0.5
MESH = pl.DeviceIdType.MESH
GROUPS = 8
HALVES = 2
FIELDS = 4
LO = 12


def kernel(nx, nz, *refs):
    it = iter(refs)
    hbm = [next(it) for _ in range(5)]
    p_out, c_out = [next(it) for _ in range(2)]
    t_in, c_in, f_in, k_in, m_in = staged = [next(it) for _ in range(5)]
    o_pm, o_liq, strip = [next(it) for _ in range(3)]
    stat, cc, pa, pb, ra, rb, cr = [next(it) for _ in range(7)]
    axp, axm, ays, ayr, azp, azm, srcn, bb, gr, rh = [next(it) for _ in range(10)]
    cxp, cys, cyr, cz, lift, rl, tt = [next(it) for _ in range(7)]
    wts, hz, off, tt0 = [next(it) for _ in range(4)]
    xs, xr, zs, zr, es, er, ts, tr = [next(it) for _ in range(8)]
    sxs, sxr, szs, szr, ses, ser = [next(it) for _ in range(6)]
    send_sem, recv_sem, st_send, st_recv, in_sem = [next(it) for _ in range(5)]

    ny, n, lanes = t_in.shape
    wide = n + 2 * W
    per = lanes // GROUPS
    fine = stat.shape[2]
    mid = LO + W
    blocks = n // 8
    gravity = 4.0 / (nz * lanes)
    half = 0.5 * gravity
    ix, iz = lax.axis_index("gx"), lax.axis_index("gz")
    f32, bf16 = jnp.float32, jnp.bfloat16
    PERM, TEMP, LIQ, CONC = range(FIELDS)

    def inside(dx, dz):
        return (ix + dx >= 0) & (ix + dx < nx) & (iz + dz >= 0) & (iz + dz < nz)

    partners = [(dx, dz) for dz in range(-1, nz) for dx in (-1, 0, 1) if (dx, dz) != (0, 0)]

    def remote(src, dst, send, recv, dx, dz):
        return dx, dz, pltpu.make_async_remote_copy(
            src_ref=src, dst_ref=dst, send_sem=send, recv_sem=recv,
            device_id={"gx": ix + dx, "gz": iz + dz}, device_id_type=MESH)

    near = [(dx, dz) for dx, dz in partners if dz <= 1]

    def halo_copies(s):
        out = []
        for m, (dx, dz) in enumerate(near):
            a, b = (1, 0) if dx > 0 else (0, 1)
            side = 0 if dz > 0 else 1
            if dz == 0:
                src, dst = xs.at[s, a], xr.at[s, b]
            elif dx == 0:
                src, dst = zs.at[s], zr.at[s, side]
            else:
                src, dst = es.at[s, a], er.at[s, b, side]
            out.append(remote(src, dst, send_sem.at[s, m], recv_sem.at[s, m], dx, dz))
        return out

    def total_copies(s):
        below = [(dx, dz) for dx, dz in partners if dz > 0]
        return [remote(ts.at[s], tr.at[s, 1 - dx, dz - 1], send_sem.at[s, len(near) + m], recv_sem.at[s, len(near) + m],
                       dx, dz) for m, (dx, dz) in enumerate(below)]

    def static_copies(along_x):
        out = []
        for m, (dx, dz) in enumerate(near):
            a, b = (1, 0) if dx > 0 else (0, 1)
            side = 0 if dz > 0 else 1
            if dz == 0:
                src, dst = sxs.at[a], sxr.at[b]
            elif dx == 0:
                src, dst = szs, szr.at[side]
            else:
                src, dst = ses.at[a], ser.at[b, side]
            if (dz == 0) == along_x:
                out.append(remote(src, dst, st_send.at[m], st_recv.at[m], dx, dz))
        return out

    def start(copies):
        for dx, dz, c in copies:
            pl.when(inside(dx, dz))(c.start)

    def arrive(copies):
        for dx, dz, c in copies:
            pl.when(inside(-dx, -dz))(c.wait_recv)

    def sent(copies):
        for dx, dz, c in copies:
            pl.when(inside(dx, dz))(c.wait_send)

    loads = [pltpu.make_async_copy(a, b, in_sem.at[i]) for i, (a, b) in enumerate(zip(hbm, staged))]
    for load in loads:
        load.start()

    for ref in (xr, zr, er, tr, sxr, szr, ser):
        ref[...] = jnp.zeros_like(ref)
    barrier = pltpu.get_barrier_semaphore()
    count = 0
    for dx, dz in partners:
        @pl.when(inside(-dx, -dz))
        def _(dx=dx, dz=dz):
            pl.semaphore_signal(barrier, inc=1, device_id={"gx": ix - dx, "gz": iz - dz}, device_id_type=MESH)
        count = count + inside(dx, dz).astype(jnp.int32)

    def lane(rows):
        return lax.broadcasted_iota(jnp.int32, (rows, lanes), 1)

    def split(value):
        high = value.astype(bf16)
        low = (value - high.astype(f32)).astype(bf16)
        return jnp.concatenate([high, low], axis=1)

    r2 = lax.broadcasted_iota(jnp.int32, (2 * lanes, lanes), 0) % lanes
    c2 = lax.broadcasted_iota(jnp.int32, (2 * lanes, lanes), 1)
    same = (r2 // per) == (c2 // per)
    wts[0:2 * lanes] = jnp.where(same, jnp.where(r2 < c2, 1.0, 0.0), 0.0).astype(bf16)
    wts[2 * lanes:4 * lanes] = jnp.where(same, 1.0, 0.0).astype(bf16)

    zrows = jnp.zeros((8, lanes), f32)
    for h in range(HALVES):
        for z in range(fine):
            for r in (LO - 4, LO + wide - 4):
                stat[PERM, h, z, r:r + 8] = zrows
                pa[h, z + 1, r:r + 8] = zrows
                pb[h, z + 1, r:r + 8] = zrows

    for load in loads:
        load.wait()
    center = pl.ds(mid, n)
    window = pl.ds(LO, wide)
    top, bottom = pl.ds(LO, W), pl.ds(mid + n, W)

    ln = lane(n)
    packed = [jnp.zeros((n, lanes), f32)] * FIELDS
    for y in range(ny):
        mark, t, c = m_in[y], t_in[y], c_in[y]
        liq = jnp.where(mark == 1, 1.0, jnp.where(mark == 2, 0.0, f_in[y]))
        solid = 1.0 - liq
        pm = k_in[y] * (liq * liq * liq / (solid * solid + 0.25) + 0.02)
        o_pm[y] = pm
        o_liq[y] = liq
        for f, v in enumerate((pm, t, liq, c)):
            strip[f, y, 0:W] = v[0:W]
            strip[f, y, W:2 * W] = v[n - W:n]
            packed[f] = jnp.where(ln // (2 * W) == y, pltpu.roll(v, (y * 2 * W + W) % lanes, 1), packed[f])
    for f in range(FIELDS):
        szs[f] = packed[f]
        ses[0, f] = packed[f][0:W]
        ses[1, f] = packed[f][n - W:n]
    pl.semaphore_wait(barrier, count)
    start(static_copies(False))

    def spread(get, put, rows):
        lw = lane(rows)
        res, grp, zc = (lw + W) % fine, lw // per, lw % per
        for h in range(HALVES):
            vals = [get(HALVES * g + h) for g in range(GROUPS)]
            moved = []
            for d in range(fine):
                comb = vals[0]
                for g in range(1, GROUPS):
                    comb = jnp.where(res == (g + d) % fine, vals[g], comb)
                z = fine * zc + (grp + d) % fine - W
                moved.append(jnp.take_along_axis(comb, jnp.clip(z, 0, lanes - 1), axis=1, mode="promise_in_bounds"))
            for z in range(fine):
                v = moved[z]
                for g in range(1, GROUPS):
                    v = jnp.where(grp == g, moved[(z - g) % fine], v)
                zw = fine * zc + z
                put(h, z, jnp.where((zw >= W) & (zw < W + lanes), v, 0.0))

    def gathered(get, put, rows):
        lw = lane(rows)
        res, grp = (lw + W) % fine, lw // per
        for h in range(HALVES):
            vals = [get(h, z) for z in range(fine)]
            moved = []
            for d in range(fine):
                comb = vals[d]
                for g in range(1, GROUPS):
                    comb = jnp.where(grp == g, vals[(g + d) % fine], comb)
                g = jnp.minimum((res - d + fine) % fine, GROUPS - 1)
                moved.append(jnp.take_along_axis(comb, g * per + (lw + W) // fine, axis=1, mode="promise_in_bounds"))
            for g in range(GROUPS):
                v = moved[0]
                for d in range(1, fine):
                    v = jnp.where(res == (g + d) % fine, moved[d], v)
                put(HALVES * g + h, v)

    for f in range(FIELDS):
        def put(h, z, v, f=f):
            sxs[0, f, h, z] = v[0:W]
            sxs[1, f, h, z] = v[W:2 * W]
        spread(lambda y, f=f: strip[f, y], put, 2 * W)
    start(static_copies(True))

    def cells(f):
        return cc.at[0] if f == CONC else stat.at[f]

    for f, ref in ((CONC, c_in), (TEMP, t_in), (PERM, o_pm), (LIQ, o_liq)):
        for r in range(0, n, 16):
            def put(h, z, v, f=f, r=r):
                cells(f)[h, z, mid + r:mid + r + 16, :] = v
            spread(lambda y, ref=ref, r=r: ref[y, r:r + 16], put, 16)

    def own_sum(values):
        zc = lane(n) % per
        out = jnp.zeros((n, lanes), f32)
        for first in sorted({0, W % fine, (W + lanes) % fine}):
            last = min([e for e in (W % fine, (W + lanes) % fine, fine) if e > first])
            part = values[first]
            for z in range(first + 1, last):
                part = part + values[z]
            zw = fine * zc + first
            out = out + jnp.where((zw >= W) & (zw < W + lanes), part, 0.0)
        return out

    def send_totals(s, sums):
        both = jnp.concatenate([split(tt0[h] + 0.2 * sums[h]) for h in range(HALVES)], axis=0)
        tot = jnp.dot(both, wts[2 * lanes:4 * lanes], preferred_element_type=f32)
        slot = lane(8) % per
        out = jnp.zeros((8, lanes), f32)
        for i in range(HALVES * blocks):
            out = jnp.where(slot == i, tot[8 * i:8 * i + 8], out)
        ts[s] = out
        start(total_copies(s))

    def edge(h, rows):
        return lane(rows) < per if h == 0 else lane(rows) >= lanes - per

    shift = (per, lanes - per)

    def turn(s):
        for h in range(HALVES):
            for z in range(fine):
                cr[h, z] = jnp.where(edge(h, n), 0.0, pltpu.roll(cc[s, 1 - h, z, center, :], shift[h], 1))

    for h in range(HALVES):
        tt0[h] = own_sum([1.0 - 0.3 * stat[TEMP, h, z, center, :] for z in range(fine)])
    send_totals(0, [own_sum([cc[0, h, z, center, :] for z in range(fine)]) for h in range(HALVES)])
    turn(0)

    zc_w = lane(wide) % per

    def insert(dst, strips, packed):
        for h in range(HALVES):
            for z in range(fine):
                dst[h, z, top, :] = strips(0, h, z)
                dst[h, z, bottom, :] = strips(1, h, z)
            for k in range(2 * W):
                at, z = divmod(k if k < W else lanes + k, fine)
                moved = pltpu.roll(packed, (at - h * 2 * W - k) % lanes, 1)
                dst[h, z, window, :] = jnp.where(zc_w == at, moved, dst[h, z, window, :])

    k_n, k_e = lane(n) % (2 * W), lane(W) % (2 * W)

    arrive(static_copies(False))
    arrive(static_copies(True))
    for f in range(FIELDS):
        hz[0:W] = jnp.where(k_e < W, ser[0, 0, f], ser[0, 1, f])
        hz[W:W + n] = jnp.where(k_n < W, szr[0, f], szr[1, f])
        hz[W + n:wide] = jnp.where(k_e < W, ser[1, 0, f], ser[1, 1, f])
        insert(cells(f), lambda b, h, z, f=f: sxr[b, f, h, z], hz[...])

    up_rows, down_rows = pl.ds(LO + 1, wide), pl.ds(LO - 1, wide)
    for h in range(HALVES):
        for z in range(fine):
            pm = stat[PERM, h, z, window, :]
            over = stat[PERM, h, z + 1, window, :] if z < fine - 1 else pltpu.roll(stat[PERM, h, 0, window, :], lanes - 1, 1)
            under = stat[PERM, h, z - 1, window, :] if z > 0 else pltpu.roll(stat[PERM, h, fine - 1, window, :], 1, 1)
            cross = jnp.where(edge(h, wide), 0.0, pltpu.roll(stat[PERM, 1 - h, z, window, :], shift[h], 1))
            c = [0.5 * (pm + other) for other in (
                stat[PERM, h, z, up_rows, :], stat[PERM, h, z, down_rows, :], stat[PERM, 1 - h, z, window, :], cross, over, under)]
            total = c[0] + c[1] + c[2] + c[3] + c[4] + c[5]
            real = pm > 0.0
            inv = jnp.where(real, 1.0 / jnp.where(real, total, 1.0), 0.0)
            cxp[h, z, window, :] = c[0]
            if h == 0:
                cys[z, window, :] = c[2]
            cyr[h, z, window, :] = c[3]
            cz[h, z + 1, window, :] = c[4]
            if z == 0:
                cz[h, 0, window, :] = c[5]
            axp[h, z] = c[0] * inv
            axm[h, z] = c[1] * inv
            ays[h, z] = c[2] * inv
            ayr[h, z] = jnp.where(edge(h, wide), 0.0, c[3] * inv)
            azp[h, z] = c[4] * inv
            azm[h, z] = c[5] * inv
            liq, t = stat[LIQ, h, z, window, :], stat[TEMP, h, z, window, :]
            srcn[h, z] = 2.0 * liq * (1.0 - liq) * t * inv
            tt[h, z] = jnp.where(real, 1.0 - 0.3 * t, 0.0)
            gr[h, z] = jnp.where(real, gravity, 0.0)
            zw = fine * (lane(n) % per) + z
            rl[h, z] = jnp.where((zw >= W) & (zw < W + lanes), SOLUTE_RATE / (stat[LIQ, h, z, center, :] + 0.1), 0.0)

    def keep(p, r, h, z, v):
        p[h, z + 1, window, :] = v
        r[1 - h, z] = pltpu.roll(v, shift[1 - h], 1)
        if z == 0:
            p[h, fine + 1, window, :] = pltpu.roll(v, lanes - 1, 1)
        if z == fine - 1:
            p[h, 0, window, :] = pltpu.roll(v, 1, 1)

    order = [0, fine - 1] + list(range(1, fine - 1))

    def carried(flow, own, other):
        return flow * jnp.where(flow > 0.0, own, other)

    up_c, down_c = pl.ds(mid + 1, n), pl.ds(mid - 1, n)

    def step(s, final):
        if not isinstance(s, int) or s > 0:
            arrive(halo_copies(s))
            hz[0:W] = jnp.where(k_e < W, er[s, 0, 0], er[s, 0, 1])
            hz[W:W + n] = jnp.where(k_n < W, zr[s, 0], zr[s, 1])
            hz[W + n:wide] = jnp.where(k_e < W, er[s, 1, 0], er[s, 1, 1])
            insert(cc.at[s], lambda b, h, z: xr[s, b, h, z], hz[...])
        sums = []
        for h in range(HALVES):
            for z in range(fine):
                rh[h, z] = tt[h, z] + 0.2 * cc[s, h, z, window, :]
            before = rh[h, 0]
            for z in range(1, W):
                before = before + rh[h, z]
            run = jnp.where(zc_w == 0, -before, 0.0)
            for z in range(fine):
                rho = rh[h, z]
                pa[h, z + 1, window, :] = run + 0.5 * rho
                run = run + rho
            sums.append(run)
            lo = half * (pltpu.roll(rh[h, fine - 1], 1, 1) + rh[h, 0])
            lift[h, 0, window, :] = lo
            for z in range(fine):
                other = rh[h, z + 1] if z < fine - 1 else pltpu.roll(rh[h, 0], lanes - 1, 1)
                hi = half * (rh[h, z] + other)
                lift[h, z + 1, window, :] = hi
                bb[h, z] = srcn[h, z] - azp[h, z] * hi + azm[h, z] * lo
                lo = hi
        arrive(total_copies(s))
        total = [tr[s, side, 0] for side in range(3)]
        for d in range(1, nz - 1):
            total = [total[side] + tr[s, side, d] for side in range(3)]
        slot = lane(8) % per
        for h in range(HALVES):
            off[h, 0:W] = jnp.where(slot == h * blocks + blocks - 1, total[0], 0.0)[8 - W:8]
            for j in range(blocks):
                off[h, W + 8 * j:W + 8 * j + 8] = jnp.where(slot == h * blocks + j, total[1], 0.0)
            off[h, W + n:wide] = jnp.where(slot == h * blocks, total[2], 0.0)[0:W]
        both = jnp.concatenate([jnp.concatenate([split(sums[h]), split(off[h])], axis=1) for h in range(HALVES)], axis=0)
        above = jnp.dot(both, wts[...], preferred_element_type=f32)
        for z in order:
            for h in range(HALVES):
                keep(pa, ra, h, z, gr[h, z] * (pa[h, z + 1, window, :] + above[h * wide:(h + 1) * wide]))

        old, new, rold, rnew = pa, pb, ra, rb
        for sweep in range(SWEEPS):
            for z in order:
                for h in range(HALVES):
                    v = bb[h, z] + axp[h, z] * old[h, z + 1, up_rows, :] + axm[h, z] * old[h, z + 1, down_rows, :]
                    v = v + (ays[h, z] * old[1 - h, z + 1, window, :] + ayr[h, z] * rold[h, z])
                    v = v + (azp[h, z] * old[h, z + 2, window, :] + azm[h, z] * old[h, z, window, :])
                    keep(new, rnew, h, z, v)
            old, new, rold, rnew = new, old, rnew, rold

        slab = jnp.zeros((n, lanes), f32)
        k_slab = lane(n) % per
        fresh_all = [[], []]
        wrap = [(pltpu.roll(cc[s, h, fine - 1, center, :], 1, 1), pltpu.roll(cc[s, h, 0, center, :], lanes - 1, 1))
                for h in range(HALVES)]
        low = [carried(cz[h, 0, center, :] * (old[h, 0, center, :] - old[h, 1, center, :] + lift[h, 0, center, :]),
                       wrap[h][0], cc[s, h, 0, center, :]) for h in range(HALVES)]
        inner = pl.ds(W, n)
        for z in range(fine):
            ps = [old[h, z + 1, center, :] for h in range(HALVES)]
            cs = [cc[s, h, z, center, :] for h in range(HALVES)]
            between = carried(cys[z, center, :] * (ps[0] - ps[1]), cs[0], cs[1])
            for h in range(HALVES):
                p, c = ps[h], cs[h]
                change = carried(cxp[h, z, center, :] * (p - old[h, z + 1, up_c, :]), c, cc[s, h, z, up_c, :])
                change = change + carried(cxp[h, z, down_c, :] * (p - old[h, z + 1, down_c, :]), c, cc[s, h, z, down_c, :])
                side = jnp.where(edge(h, n), 0.0, rold[h, z, inner, :])
                change = change + carried(cyr[h, z, center, :] * (p - side), c, cr[h, z])
                change = change + between if h == 0 else change - between
                over = cc[s, h, z + 1, center, :] if z < fine - 1 else wrap[h][1]
                high = carried(cz[h, z + 1, center, :] * (p - old[h, z + 2, center, :] + lift[h, z + 1, center, :]), c, over)
                change = change + (high - low[h])
                low[h] = high
                fresh = c - rl[h, z] * change
                cc[s + 1, h, z, center, :] = fresh
                if not final:
                    xs[s + 1, 0, h, z] = fresh[0:W]
                    xs[s + 1, 1, h, z] = fresh[n - W:n]
                    for j in range(2 * W):
                        at, zj = divmod(lanes + j if j < W else j, fine)
                        if zj == z:
                            k = h * 2 * W + j
                            slab = jnp.where(k_slab == k, pltpu.roll(fresh, (k - at) % lanes, 1), slab)
        if not final:
            zs[s + 1] = slab
            es[s + 1, 0] = slab[0:W]
            es[s + 1, 1] = slab[n - W:n]
            start(halo_copies(s + 1))
            send_totals(s + 1, [own_sum([cc[s + 1, h, z, center, :] for z in range(fine)]) for h in range(HALVES)])
            turn(s + 1)
        else:
            for r in range(0, n, 16):
                def put_p(y, v, r=r):
                    p_out[y, r:r + 16] = v

                def put_c(y, v, r=r):
                    c_out[y, r:r + 16] = v
                gathered(lambda h, z, r=r: old[h, z + 1, mid + r:mid + r + 16, :], put_p, 16)
                gathered(lambda h, z, r=r: cc[s + 1, h, z, mid + r:mid + r + 16, :], put_c, 16)

    for s in range(STEPS):
        step(s, s == STEPS - 1)

    sent(static_copies(False))
    sent(static_copies(True))
    for s in range(STEPS):
        if s > 0:
            sent(halo_copies(s))
        sent(total_copies(s))


def on_device(nx, nz, *args):
    ny, n, lanes = args[0].shape
    wide = n + 2 * W
    rows = wide + 2 * LO
    per = lanes // GROUPS
    fine = -(-(lanes + 2 * W) // per)
    copies = 8 + 3 * (nz - 1)

    def vmem(*shape):
        return pltpu.VMEM(shape, jnp.float32)

    padded, plain, own = (HALVES, fine, rows, lanes), (HALVES, fine, wide, lanes), (HALVES, fine, n, lanes)
    slots = (HALVES, fine + 2, rows, lanes)
    scratch = [pltpu.VMEM((ny, n, lanes), a.dtype) for a in args]
    scratch += [vmem(ny, n, lanes)] * 2 + [vmem(FIELDS, ny, 2 * W, lanes)]
    scratch += [vmem(FIELDS - 1, *padded), vmem(STEPS + 1, *padded), vmem(*slots), vmem(*slots)]
    scratch += [vmem(*plain), vmem(*plain), vmem(*own)]
    scratch += [vmem(*plain)] * 10
    scratch += [vmem(*padded), vmem(fine, rows, lanes), vmem(*padded), vmem(HALVES, fine + 1, rows, lanes),
                vmem(HALVES, fine + 1, rows, lanes), vmem(*own), vmem(*plain)]
    scratch += [pltpu.VMEM((4 * lanes, lanes), jnp.bfloat16), vmem(wide, lanes), vmem(HALVES, wide, lanes),
                vmem(HALVES, n, lanes)]
    scratch += [vmem(STEPS, 2, HALVES, fine, W, lanes)] * 2
    scratch += [vmem(STEPS, n, lanes), vmem(STEPS, 2, n, lanes)]
    scratch += [vmem(STEPS, 2, W, lanes), vmem(STEPS, 2, 2, W, lanes)]
    scratch += [vmem(STEPS, 8, lanes), vmem(STEPS, 3, nz - 1, 8, lanes)]
    scratch += [vmem(2, FIELDS, HALVES, fine, W, lanes)] * 2
    scratch += [vmem(FIELDS, n, lanes), vmem(2, FIELDS, n, lanes), vmem(2, FIELDS, W, lanes), vmem(2, 2, FIELDS, W, lanes)]
    scratch += [pltpu.SemaphoreType.DMA((STEPS, copies))] * 2 + [pltpu.SemaphoreType.DMA((8,))] * 2
    scratch += [pltpu.SemaphoreType.DMA((5,))]
    return tuple(pl.pallas_call(
        functools.partial(kernel, nx, nz),
        out_shape=[jax.ShapeDtypeStruct((ny, n, lanes), jnp.float32)] * 2,
        in_specs=[pl.BlockSpec(memory_space=pltpu.HBM)] * 5,
        out_specs=[pl.BlockSpec(memory_space=pltpu.VMEM)] * 2,
        scratch_shapes=scratch,
        compiler_params=pltpu.CompilerParams(
            collective_id=0, has_side_effects=True, vmem_limit_bytes=63 * 1024 * 1024),
    )(*args))


def solution(mesh):
    placed = P(None, "gx", "gz")
    return jax.shard_map(
        functools.partial(on_device, mesh.shape["gx"], mesh.shape["gz"]),
        mesh=mesh,
        in_specs=(placed,) * 5,
        out_specs=(placed, placed),
        check_vma=False,
    )
```

time: 58 us -> 39.7 us (0.68)
  the two profiles are of different devices: /device:TPU:9 before, /device:TPU:5 now
where the time goes in v1:
time: 39.7 us; the launch traced here: 39.5 us
  Pallas kernels  36.3 us (91%)
  local copies, waits for them, and re-layouts  2.57 us (6%)
  between operations  0.65 us (2%)
    pallas_call x1, Pallas kernels, on_device(): pl.pallas_call(functools.partial(kernel, nx, nz), out_shape=[jax.ShapeDty...  36.3 us
    unnamed x4, local copies, waits for them, and re-layouts  2.57 us

profile of v1, /device:TPU:5, one launch (start us, length us, event | category | flops | bytes accessed | tf_op | source)
XLA Modules:
  0.0 39.5 jit_solution(929342485810032876)
XLA Ops:
  0.6 36.3 %shard_map.68 = (f32[16,48,128]{2,1,0:T(8,128)}, f32[16,48,128]{2,1,0:T(8,128)}) custom-call(f32[16,48,128]{2,1,0:T(8,128)} %refs_0_.1, f32[16,48,128]{2,1,0:T(8,128)} %refs_1_.1, f32[16,48,128]{2,1,0:T(8,128)} %refs_2_.1, f32[16,48,128]{2,1,0:T(8,128)} %refs_3_.1, s32[16,48,128]{2,1,0:T(8,128)} %refs_4_.1), custom_call_target="tpu_custom_call" | custom-call | tf_op jit(solution)/shard_map/pallas_call | solution.py:471
  36.9 0.0 copy-start
  37.0 1.8 %copy.9 = f32[16,48,128]{2,1,0:T(8,128)} copy(f32[16,48,128]{2,1,0:T(8,128)} %get-tuple-element.4) | data formatting | bytes 786432
  38.8 0.0 copy-done
  38.8 0.7 %copy.10 = f32[16,48,128]{2,1,0:T(8,128)} copy(f32[16,48,128]{2,1,0:T(8,128)S(1)} %copy-done) | data formatting | bytes 786432
Async XLA Ops:
  36.9 1.8 %copy-start = (f32[16,48,128]{2,1,0:T(8,128)S(1)}, f32[16,48,128]{2,1,0:T(8,128)}, u32[]{:S(2)}) copy-start(f32[16,48,128]{2,1,0:T(8,128)} %get-tuple-element.5) | copy-start | bytes 1179652

commit v2 on v1

--- a/solution.py
+++ b/solution.py
@@ -16,6 +16,7 @@
 HALVES = 2
 FIELDS = 4
 LO = 12
+PART = 16
 
 
 def kernel(nx, nz, *refs):
@@ -30,7 +31,7 @@
     wts, hz, off, tt0 = [next(it) for _ in range(4)]
     xs, xr, zs, zr, es, er, ts, tr = [next(it) for _ in range(8)]
     sxs, sxr, szs, szr, ses, ser = [next(it) for _ in range(6)]
-    send_sem, recv_sem, st_send, st_recv, in_sem = [next(it) for _ in range(5)]
+    send_sem, recv_sem, st_send, st_recv, in_sem, out_sem = [next(it) for _ in range(6)]
 
     ny, n, lanes = t_in.shape
     wide = n + 2 * W
@@ -56,7 +57,7 @@
 
     near = [(dx, dz) for dx, dz in partners if dz <= 1]
 
-    def halo_copies(s):
+    def halo_copies(s, along_x):
         out = []
         for m, (dx, dz) in enumerate(near):
             a, b = (1, 0) if dx > 0 else (0, 1)
@@ -67,8 +68,9 @@
                 src, dst = zs.at[s], zr.at[s, side]
             else:
                 src, dst = es.at[s, a], er.at[s, b, side]
-            out.append(remote(src, dst, send_sem.at[s, m], recv_sem.at[s, m], dx, dz))
-        return out
+            if (dx != 0) == along_x:
+                out.append(remote(src, dst, send_sem.at[s, m], recv_sem.at[s, m], dx, dz))
+        return sorted(out, key=lambda item: item[1] != 0)
 
     def total_copies(s):
         below = [(dx, dz) for dx, dz in partners if dz > 0]
@@ -86,9 +88,9 @@
                 src, dst = szs, szr.at[side]
             else:
                 src, dst = ses.at[a], ser.at[b, side]
-            if (dz == 0) == along_x:
+            if (dx != 0) == along_x:
                 out.append(remote(src, dst, st_send.at[m], st_recv.at[m], dx, dz))
-        return out
+        return sorted(out, key=lambda item: item[1] != 0)
 
     def start(copies):
         for dx, dz, c in copies:
@@ -183,24 +185,6 @@
                 zw = fine * zc + z
                 put(h, z, jnp.where((zw >= W) & (zw < W + lanes), v, 0.0))
 
-    def gathered(get, put, rows):
-        lw = lane(rows)
-        res, grp = (lw + W) % fine, lw // per
-        for h in range(HALVES):
-            vals = [get(h, z) for z in range(fine)]
-            moved = []
-            for d in range(fine):
-                comb = vals[d]
-                for g in range(1, GROUPS):
-                    comb = jnp.where(grp == g, vals[(g + d) % fine], comb)
-                g = jnp.minimum((res - d + fine) % fine, GROUPS - 1)
-                moved.append(jnp.take_along_axis(comb, g * per + (lw + W) // fine, axis=1, mode="promise_in_bounds"))
-            for g in range(GROUPS):
-                v = moved[0]
-                for d in range(1, fine):
-                    v = jnp.where(res == (g + d) % fine, moved[d], v)
-                put(HALVES * g + h, v)
-
     for f in range(FIELDS):
         def put(h, z, v, f=f):
             sxs[0, f, h, z] = v[0:W]
@@ -256,57 +240,76 @@
 
     zc_w = lane(wide) % per
 
-    def insert(dst, strips, packed):
-        for h in range(HALVES):
-            for z in range(fine):
-                dst[h, z, top, :] = strips(0, h, z)
-                dst[h, z, bottom, :] = strips(1, h, z)
+    def insert(dst, packed, row, rows):
+        zc, at_rows = lane(rows) % per, pl.ds(LO + row, rows)
+        for h in range(HALVES):
             for k in range(2 * W):
                 at, z = divmod(k if k < W else lanes + k, fine)
                 moved = pltpu.roll(packed, (at - h * 2 * W - k) % lanes, 1)
-                dst[h, z, window, :] = jnp.where(zc_w == at, moved, dst[h, z, window, :])
+                dst[h, z, at_rows, :] = jnp.where(zc == at, moved, dst[h, z, at_rows, :])
+
+    def insert_strips(dst, strips, corners):
+        for h in range(HALVES):
+            for z in range(fine):
+                dst[h, z, top, :] = strips(0, h, z)
+                dst[h, z, bottom, :] = strips(1, h, z)
+        for b in range(2):
+            hz[b] = jnp.where(k_e < W, corners(b, 0), corners(b, 1))
+            insert(dst, hz[b], b * (n + W), W)
 
     k_n, k_e = lane(n) % (2 * W), lane(W) % (2 * W)
 
     arrive(static_copies(False))
+    for f in range(FIELDS):
+        insert(cells(f), jnp.where(k_n < W, szr[0, f], szr[1, f]), W, n)
+
+    up_rows, down_rows = pl.ds(LO + 1, wide), pl.ds(LO - 1, wide)
+
+    def coefficients(row, rows):
+        here, up, down, flat = pl.ds(LO + row, rows), pl.ds(LO + row + 1, rows), pl.ds(LO + row - 1, rows), pl.ds(row, rows)
+        beside = [edge(h, rows) for h in range(HALVES)]
+        for h in range(HALVES):
+            for z in range(fine):
+                pm = stat[PERM, h, z, here, :]
+                over = stat[PERM, h, z + 1, here, :] if z < fine - 1 else pltpu.roll(stat[PERM, h, 0, here, :], lanes - 1, 1)
+                under = stat[PERM, h, z - 1, here, :] if z > 0 else pltpu.roll(stat[PERM, h, fine - 1, here, :], 1, 1)
+                cross = jnp.where(beside[h], 0.0, pltpu.roll(stat[PERM, 1 - h, z, here, :], shift[h], 1))
+                c = [0.5 * (pm + other) for other in (
+                    stat[PERM, h, z, up, :], stat[PERM, h, z, down, :], stat[PERM, 1 - h, z, here, :], cross, over, under)]
+                total = c[0] + c[1] + c[2] + c[3] + c[4] + c[5]
+                real = pm > 0.0
+                inv = jnp.where(real, 1.0 / jnp.where(real, total, 1.0), 0.0)
+                cxp[h, z, here, :] = c[0]
+                if h == 0:
+                    cys[z, here, :] = c[2]
+                cyr[h, z, here, :] = c[3]
+                cz[h, z + 1, here, :] = c[4]
+                if z == 0:
+                    cz[h, 0, here, :] = c[5]
+                axp[h, z, flat] = c[0] * inv
+                axm[h, z, flat] = c[1] * inv
+                ays[h, z, flat] = c[2] * inv
+                ayr[h, z, flat] = jnp.where(beside[h], 0.0, c[3] * inv)
+                azp[h, z, flat] = c[4] * inv
+                azm[h, z, flat] = c[5] * inv
+                liq, t = stat[LIQ, h, z, here, :], stat[TEMP, h, z, here, :]
+                srcn[h, z, flat] = 2.0 * liq * (1.0 - liq) * t * inv
+                tt[h, z, flat] = jnp.where(real, 1.0 - 0.3 * t, 0.0)
+                gr[h, z, flat] = jnp.where(real, gravity, 0.0)
+
+    zc_n = lane(n) % per
+    for h in range(HALVES):
+        for z in range(fine):
+            zw = fine * zc_n + z
+            rl[h, z] = jnp.where((zw >= W) & (zw < W + lanes), SOLUTE_RATE / (stat[LIQ, h, z, center, :] + 0.1), 0.0)
+    coefficients(8, wide - 16)
+    sent(static_copies(False))
     arrive(static_copies(True))
     for f in range(FIELDS):
-        hz[0:W] = jnp.where(k_e < W, ser[0, 0, f], ser[0, 1, f])
-        hz[W:W + n] = jnp.where(k_n < W, szr[0, f], szr[1, f])
-        hz[W + n:wide] = jnp.where(k_e < W, ser[1, 0, f], ser[1, 1, f])
-        insert(cells(f), lambda b, h, z, f=f: sxr[b, f, h, z], hz[...])
-
-    up_rows, down_rows = pl.ds(LO + 1, wide), pl.ds(LO - 1, wide)
-    for h in range(HALVES):
-        for z in range(fine):
-            pm = stat[PERM, h, z, window, :]
-            over = stat[PERM, h, z + 1, window, :] if z < fine - 1 else pltpu.roll(stat[PERM, h, 0, window, :], lanes - 1, 1)
-            under = stat[PERM, h, z - 1, window, :] if z > 0 else pltpu.roll(stat[PERM, h, fine - 1, window, :], 1, 1)
-            cross = jnp.where(edge(h, wide), 0.0, pltpu.roll(stat[PERM, 1 - h, z, window, :], shift[h], 1))
-            c = [0.5 * (pm + other) for other in (
-                stat[PERM, h, z, up_rows, :], stat[PERM, h, z, down_rows, :], stat[PERM, 1 - h, z, window, :], cross, over, under)]
-            total = c[0] + c[1] + c[2] + c[3] + c[4] + c[5]
-            real = pm > 0.0
-            inv = jnp.where(real, 1.0 / jnp.where(real, total, 1.0), 0.0)
-            cxp[h, z, window, :] = c[0]
-            if h == 0:
-                cys[z, window, :] = c[2]
-            cyr[h, z, window, :] = c[3]
-            cz[h, z + 1, window, :] = c[4]
-            if z == 0:
-                cz[h, 0, window, :] = c[5]
-            axp[h, z] = c[0] * inv
-            axm[h, z] = c[1] * inv
-            ays[h, z] = c[2] * inv
-            ayr[h, z] = jnp.where(edge(h, wide), 0.0, c[3] * inv)
-            azp[h, z] = c[4] * inv
-            azm[h, z] = c[5] * inv
-            liq, t = stat[LIQ, h, z, window, :], stat[TEMP, h, z, window, :]
-            srcn[h, z] = 2.0 * liq * (1.0 - liq) * t * inv
-            tt[h, z] = jnp.where(real, 1.0 - 0.3 * t, 0.0)
-            gr[h, z] = jnp.where(real, gravity, 0.0)
-            zw = fine * (lane(n) % per) + z
-            rl[h, z] = jnp.where((zw >= W) & (zw < W + lanes), SOLUTE_RATE / (stat[LIQ, h, z, center, :] + 0.1), 0.0)
+        insert_strips(cells(f), lambda b, h, z, f=f: sxr[b, f, h, z], lambda b, side, f=f: ser[b, side, f])
+    for row in (0, wide - 8):
+        coefficients(row, 8)
+    sent(static_copies(True))
 
     def keep(p, r, h, z, v):
         p[h, z + 1, window, :] = v
@@ -321,15 +324,15 @@
     def carried(flow, own, other):
         return flow * jnp.where(flow > 0.0, own, other)
 
-    up_c, down_c = pl.ds(mid + 1, n), pl.ds(mid - 1, n)
-
     def step(s, final):
-        if not isinstance(s, int) or s > 0:
-            arrive(halo_copies(s))
-            hz[0:W] = jnp.where(k_e < W, er[s, 0, 0], er[s, 0, 1])
-            hz[W:W + n] = jnp.where(k_n < W, zr[s, 0], zr[s, 1])
-            hz[W + n:wide] = jnp.where(k_e < W, er[s, 1, 0], er[s, 1, 1])
-            insert(cc.at[s], lambda b, h, z: xr[s, b, h, z], hz[...])
+        if s > 0:
+            sent(halo_copies(s, True))
+            sent(halo_copies(s, False))
+            sent(total_copies(s))
+            arrive(halo_copies(s, False))
+            insert(cc.at[s], jnp.where(k_n < W, zr[s, 0], zr[s, 1]), W, n)
+            arrive(halo_copies(s, True))
+            insert_strips(cc.at[s], lambda b, h, z: xr[s, b, h, z], lambda b, side: er[s, b, side])
         sums = []
         for h in range(HALVES):
             for z in range(fine):
@@ -351,6 +354,8 @@
                 lift[h, z + 1, window, :] = hi
                 bb[h, z] = srcn[h, z] - azp[h, z] * hi + azm[h, z] * lo
                 lo = hi
+        if s == 0:
+            sent(total_copies(0))
         arrive(total_copies(s))
         total = [tr[s, side, 0] for side in range(3)]
         for d in range(1, nz - 1):
@@ -377,65 +382,107 @@
                     keep(new, rnew, h, z, v)
             old, new, rold, rnew = new, old, rnew, rold
 
-        slab = jnp.zeros((n, lanes), f32)
-        k_slab = lane(n) % per
-        fresh_all = [[], []]
-        wrap = [(pltpu.roll(cc[s, h, fine - 1, center, :], 1, 1), pltpu.roll(cc[s, h, 0, center, :], lanes - 1, 1))
-                for h in range(HALVES)]
-        low = [carried(cz[h, 0, center, :] * (old[h, 0, center, :] - old[h, 1, center, :] + lift[h, 0, center, :]),
-                       wrap[h][0], cc[s, h, 0, center, :]) for h in range(HALVES)]
-        inner = pl.ds(W, n)
-        for z in range(fine):
-            ps = [old[h, z + 1, center, :] for h in range(HALVES)]
-            cs = [cc[s, h, z, center, :] for h in range(HALVES)]
-            between = carried(cys[z, center, :] * (ps[0] - ps[1]), cs[0], cs[1])
-            for h in range(HALVES):
-                p, c = ps[h], cs[h]
-                change = carried(cxp[h, z, center, :] * (p - old[h, z + 1, up_c, :]), c, cc[s, h, z, up_c, :])
-                change = change + carried(cxp[h, z, down_c, :] * (p - old[h, z + 1, down_c, :]), c, cc[s, h, z, down_c, :])
-                side = jnp.where(edge(h, n), 0.0, rold[h, z, inner, :])
-                change = change + carried(cyr[h, z, center, :] * (p - side), c, cr[h, z])
-                change = change + between if h == 0 else change - between
-                over = cc[s, h, z + 1, center, :] if z < fine - 1 else wrap[h][1]
-                high = carried(cz[h, z + 1, center, :] * (p - old[h, z + 2, center, :] + lift[h, z + 1, center, :]), c, over)
-                change = change + (high - low[h])
-                low[h] = high
-                fresh = c - rl[h, z] * change
-                cc[s + 1, h, z, center, :] = fresh
-                if not final:
-                    xs[s + 1, 0, h, z] = fresh[0:W]
-                    xs[s + 1, 1, h, z] = fresh[n - W:n]
+        def transport(row, rows):
+            here, up, down = pl.ds(mid + row, rows), pl.ds(mid + row + 1, rows), pl.ds(mid + row - 1, rows)
+            flat, inner = pl.ds(row, rows), pl.ds(W + row, rows)
+            slab = jnp.zeros((rows, lanes), f32)
+            k_slab = lane(rows) % per
+            wrap = [(pltpu.roll(cc[s, h, fine - 1, here, :], 1, 1), pltpu.roll(cc[s, h, 0, here, :], lanes - 1, 1))
+                    for h in range(HALVES)]
+            low = [carried(cz[h, 0, here, :] * (old[h, 0, here, :] - old[h, 1, here, :] + lift[h, 0, here, :]),
+                           wrap[h][0], cc[s, h, 0, here, :]) for h in range(HALVES)]
+            for z in range(fine):
+                ps = [old[h, z + 1, here, :] for h in range(HALVES)]
+                cs = [cc[s, h, z, here, :] for h in range(HALVES)]
+                between = carried(cys[z, here, :] * (ps[0] - ps[1]), cs[0], cs[1])
+                for h in range(HALVES):
+                    p, c = ps[h], cs[h]
+                    change = carried(cxp[h, z, here, :] * (p - old[h, z + 1, up, :]), c, cc[s, h, z, up, :])
+                    change = change + carried(cxp[h, z, down, :] * (p - old[h, z + 1, down, :]), c, cc[s, h, z, down, :])
+                    side = jnp.where(edge(h, rows), 0.0, rold[h, z, inner, :])
+                    change = change + carried(cyr[h, z, here, :] * (p - side), c, cr[h, z, flat, :])
+                    change = change + between if h == 0 else change - between
+                    over = cc[s, h, z + 1, here, :] if z < fine - 1 else wrap[h][1]
+                    high = carried(cz[h, z + 1, here, :] * (p - old[h, z + 2, here, :] + lift[h, z + 1, here, :]), c, over)
+                    change = change + (high - low[h])
+                    low[h] = high
+                    fresh = c - rl[h, z, flat, :] * change
+                    cc[s + 1, h, z, here, :] = fresh
+                    if final:
+                        continue
+                    if row == 0:
+                        xs[s + 1, 0, h, z] = fresh[0:W]
+                    if row + rows == n:
+                        xs[s + 1, 1, h, z] = fresh[rows - W:rows]
                     for j in range(2 * W):
                         at, zj = divmod(lanes + j if j < W else j, fine)
                         if zj == z:
                             k = h * 2 * W + j
                             slab = jnp.where(k_slab == k, pltpu.roll(fresh, (k - at) % lanes, 1), slab)
+            if final:
+                return
+            zs[s + 1, flat, :] = slab
+            if row == 0:
+                es[s + 1, 0] = slab[0:W]
+            if row + rows == n:
+                es[s + 1, 1] = slab[rows - W:rows]
+
         if not final:
-            zs[s + 1] = slab
-            es[s + 1, 0] = slab[0:W]
-            es[s + 1, 1] = slab[n - W:n]
-            start(halo_copies(s + 1))
+            transport(0, 8)
+            transport(n - 8, 8)
+            start(halo_copies(s + 1, True))
+            transport(8, n - 16)
+            start(halo_copies(s + 1, False))
             send_totals(s + 1, [own_sum([cc[s + 1, h, z, center, :] for z in range(fine)]) for h in range(HALVES)])
             turn(s + 1)
         else:
-            for r in range(0, n, 16):
-                def put_p(y, v, r=r):
-                    p_out[y, r:r + 16] = v
-
-                def put_c(y, v, r=r):
-                    c_out[y, r:r + 16] = v
-                gathered(lambda h, z, r=r: old[h, z + 1, mid + r:mid + r + 16, :], put_p, 16)
-                gathered(lambda h, z, r=r: cc[s + 1, h, z, mid + r:mid + r + 16, :], put_c, 16)
+            out = pltpu.make_async_copy(old.at[:, pl.ds(1, fine), center, :], p_out, out_sem.at[0])
+            out.start()
+            transport(0, n)
+            last = pltpu.make_async_copy(cc.at[s + 1, :, :, center, :], c_out, out_sem.at[1])
+            last.start()
+            out.wait()
+            last.wait()
 
     for s in range(STEPS):
         step(s, s == STEPS - 1)
 
-    sent(static_copies(False))
-    sent(static_copies(True))
-    for s in range(STEPS):
-        if s > 0:
-            sent(halo_copies(s))
-        sent(total_copies(s))
+
+def hand_out(p, c, p_out, c_out, p_cells, c_cells, p_block, c_block, in_sem, out_sem):
+    fine, n, lanes = p.shape[1:]
+    per = lanes // GROUPS
+    parts = [pl.ds(r, PART) for r in range(0, n, PART)]
+    fields = ((p, p_cells, p_block, p_out), (c, c_cells, c_block, c_out))
+    loads = [[pltpu.make_async_copy(src.at[:, :, part, :], cells.at[:, :, part, :], in_sem.at[a, i])
+              for a, (src, cells, _, _) in enumerate(fields)] for i, part in enumerate(parts)]
+    stores = [[pltpu.make_async_copy(block.at[:, part, :], dst.at[:, part, :], out_sem.at[a, i])
+               for a, (_, _, block, dst) in enumerate(fields)] for i, part in enumerate(parts)]
+    for pair in loads:
+        for load in pair:
+            load.start()
+    ln = lax.broadcasted_iota(jnp.int32, (PART, lanes), 1)
+    res, grp = (ln + W) % fine, ln // per
+    for i, part in enumerate(parts):
+        for a, (_, cells, block, _) in enumerate(fields):
+            loads[i][a].wait()
+            for h in range(HALVES):
+                vals = [cells[h, z, part, :] for z in range(fine)]
+                moved = []
+                for d in range(fine):
+                    comb = vals[d]
+                    for g in range(1, GROUPS):
+                        comb = jnp.where(grp == g, vals[(g + d) % fine], comb)
+                    g = jnp.minimum((res - d + fine) % fine, GROUPS - 1)
+                    moved.append(jnp.take_along_axis(comb, g * per + (ln + W) // fine, axis=1, mode="promise_in_bounds"))
+                for g in range(GROUPS):
+                    v = moved[0]
+                    for d in range(1, fine):
+                        v = jnp.where(res == (g + d) % fine, moved[d], v)
+                    block[HALVES * g + h, part, :] = v
+            stores[i][a].start()
+    for pair in stores:
+        for store in pair:
+            store.wait()
 
 
 def on_device(nx, nz, *args):
@@ -458,7 +505,7 @@
     scratch += [vmem(*plain)] * 10
     scratch += [vmem(*padded), vmem(fine, rows, lanes), vmem(*padded), vmem(HALVES, fine + 1, rows, lanes),
                 vmem(HALVES, fine + 1, rows, lanes), vmem(*own), vmem(*plain)]
-    scratch += [pltpu.VMEM((4 * lanes, lanes), jnp.bfloat16), vmem(wide, lanes), vmem(HALVES, wide, lanes),
+    scratch += [pltpu.VMEM((4 * lanes, lanes), jnp.bfloat16), vmem(2, W, lanes), vmem(HALVES, wide, lanes),
                 vmem(HALVES, n, lanes)]
     scratch += [vmem(STEPS, 2, HALVES, fine, W, lanes)] * 2
     scratch += [vmem(STEPS, n, lanes), vmem(STEPS, 2, n, lanes)]
@@ -467,16 +514,24 @@
     scratch += [vmem(2, FIELDS, HALVES, fine, W, lanes)] * 2
     scratch += [vmem(FIELDS, n, lanes), vmem(2, FIELDS, n, lanes), vmem(2, FIELDS, W, lanes), vmem(2, 2, FIELDS, W, lanes)]
     scratch += [pltpu.SemaphoreType.DMA((STEPS, copies))] * 2 + [pltpu.SemaphoreType.DMA((8,))] * 2
-    scratch += [pltpu.SemaphoreType.DMA((5,))]
-    return tuple(pl.pallas_call(
+    scratch += [pltpu.SemaphoreType.DMA((5,)), pltpu.SemaphoreType.DMA((2,))]
+    cells = pl.pallas_call(
         functools.partial(kernel, nx, nz),
-        out_shape=[jax.ShapeDtypeStruct((ny, n, lanes), jnp.float32)] * 2,
+        out_shape=[jax.ShapeDtypeStruct(own, jnp.float32)] * 2,
         in_specs=[pl.BlockSpec(memory_space=pltpu.HBM)] * 5,
-        out_specs=[pl.BlockSpec(memory_space=pltpu.VMEM)] * 2,
+        out_specs=[pl.BlockSpec(memory_space=pltpu.HBM)] * 2,
         scratch_shapes=scratch,
         compiler_params=pltpu.CompilerParams(
             collective_id=0, has_side_effects=True, vmem_limit_bytes=63 * 1024 * 1024),
-    )(*args))
+    )(*args)
+    return tuple(pl.pallas_call(
+        hand_out,
+        out_shape=[jax.ShapeDtypeStruct((ny, n, lanes), jnp.float32)] * 2,
+        in_specs=[pl.BlockSpec(memory_space=pltpu.HBM)] * 2,
+        out_specs=[pl.BlockSpec(memory_space=pltpu.HBM)] * 2,
+        scratch_shapes=[vmem(*own)] * 2 + [vmem(ny, n, lanes)] * 2 + [pltpu.SemaphoreType.DMA((2, n // PART))] * 2,
+        compiler_params=pltpu.CompilerParams(vmem_limit_bytes=63 * 1024 * 1024),
+    )(*cells))
 
 
 def solution(mesh):

time: 39.7 us -> 37.2 us (0.937)
  the two profiles are of different devices: /device:TPU:5 before, /device:TPU:9 now
where the time goes in v2:
time: 37.2 us; the launch traced here: 36.4 us
  Pallas kernels  35.8 us (96%)
  between operations  0.64 us (2%)
    pallas_call x1, Pallas kernels, on_device(): pl.pallas_call(functools.partial(kernel, nx, nz), out_shape=[jax.ShapeDty...  33.2 us
    pallas_call x1, Pallas kernels, on_device(): pl.pallas_call(hand_out, out_shape=[jax.ShapeDtypeStruct((ny, n, lanes),...  2.62 us

profile of v2, /device:TPU:9, one launch (start us, length us, event | category | flops | bytes accessed | tf_op | source)
XLA Modules:
  0.0 36.4 jit_solution(3402580756234700231)
XLA Ops:
  0.6 33.2 %shard_map.68 = (f32[2,9,48,128]{3,2,1,0:T(8,128)}, f32[2,9,48,128]{3,2,1,0:T(8,128)}) custom-call(f32[16,48,128]{2,1,0:T(8,128)} %refs_0_.1, f32[16,48,128]{2,1,0:T(8,128)} %refs_1_.1, f32[16,48,128]{2,1,0:T(8,128)} %refs_2_.1, f32[16,48,128]{2,1,0:T(8,128)} %refs_3_.1, s32[16,48,128]{2,1,0:T(8,128)} %refs_4_.1), custom_call_target="tpu_custom_call" | custom-call | tf_op jit(solution)/shard_map/pallas_call | solution.py:518
  33.8 2.6 %shard_map.69 = (f32[16,48,128]{2,1,0:T(8,128)}, f32[16,48,128]{2,1,0:T(8,128)}) custom-call(f32[2,9,48,128]{3,2,1,0:T(8,128)} %get-tuple-element.4.p, f32[2,9,48,128]{3,2,1,0:T(8,128)} %get-tuple-element.5.c), custom_call_target="tpu_custom_call" | custom-call | tf_op jit(solution)/shard_map/pallas_call | solution.py:527

commit v3 on v2

--- a/solution.py
+++ b/solution.py
@@ -25,11 +25,13 @@
     p_out, c_out = [next(it) for _ in range(2)]
     t_in, c_in, f_in, k_in, m_in = staged = [next(it) for _ in range(5)]
     o_pm, o_liq, strip = [next(it) for _ in range(3)]
-    stat, cc, pa, pb, ra, rb, cr = [next(it) for _ in range(7)]
+    stat, cc, cr = [next(it) for _ in range(3)]
+    press = [next(it) for _ in range(W)]
+    turned = [next(it) for _ in range(W)]
     axp, axm, ays, ayr, azp, azm, srcn, bb, gr, rh = [next(it) for _ in range(10)]
     cxp, cys, cyr, cz, lift, rl, tt = [next(it) for _ in range(7)]
-    wts, hz, off, tt0 = [next(it) for _ in range(4)]
-    xs, xr, zs, zr, es, er, ts, tr = [next(it) for _ in range(8)]
+    wts, hz, off, sm, ab, tt0 = [next(it) for _ in range(6)]
+    xs, xr, zs, zr, es, er, ts, td, tr = [next(it) for _ in range(9)]
     sxs, sxr, szs, szr, ses, ser = [next(it) for _ in range(6)]
     send_sem, recv_sem, st_send, st_recv, in_sem, out_sem = [next(it) for _ in range(6)]
 
@@ -69,13 +71,14 @@
             else:
                 src, dst = es.at[s, a], er.at[s, b, side]
             if (dx != 0) == along_x:
-                out.append(remote(src, dst, send_sem.at[s, m], recv_sem.at[s, m], dx, dz))
+                out.append(remote(src, dst, send_sem.at[m], recv_sem.at[s, m], dx, dz))
         return sorted(out, key=lambda item: item[1] != 0)
 
-    def total_copies(s):
+    def total_copies(s, along_x):
         below = [(dx, dz) for dx, dz in partners if dz > 0]
-        return [remote(ts.at[s], tr.at[s, 1 - dx, dz - 1], send_sem.at[s, len(near) + m], recv_sem.at[s, len(near) + m],
-                       dx, dz) for m, (dx, dz) in enumerate(below)]
+        return [remote((td if along_x else ts).at[s], tr.at[s, 1 - dx, dz - 1],
+                       send_sem.at[len(near) + m], recv_sem.at[s, len(near) + m], dx, dz)
+                for m, (dx, dz) in enumerate(below) if (dx != 0) == along_x]
 
     def static_copies(along_x):
         out = []
@@ -137,8 +140,6 @@
         for z in range(fine):
             for r in (LO - 4, LO + wide - 4):
                 stat[PERM, h, z, r:r + 8] = zrows
-                pa[h, z + 1, r:r + 8] = zrows
-                pb[h, z + 1, r:r + 8] = zrows
 
     for load in loads:
         load.wait()
@@ -163,8 +164,6 @@
         szs[f] = packed[f]
         ses[0, f] = packed[f][0:W]
         ses[1, f] = packed[f][n - W:n]
-    pl.semaphore_wait(barrier, count)
-    start(static_copies(False))
 
     def spread(get, put, rows):
         lw = lane(rows)
@@ -190,7 +189,9 @@
             sxs[0, f, h, z] = v[0:W]
             sxs[1, f, h, z] = v[W:2 * W]
         spread(lambda y, f=f: strip[f, y], put, 2 * W)
+    pl.semaphore_wait(barrier, count)
     start(static_copies(True))
+    start(static_copies(False))
 
     def cells(f):
         return cc.at[0] if f == CONC else stat.at[f]
@@ -201,9 +202,9 @@
                 cells(f)[h, z, mid + r:mid + r + 16, :] = v
             spread(lambda y, ref=ref, r=r: ref[y, r:r + 16], put, 16)
 
-    def own_sum(values):
-        zc = lane(n) % per
-        out = jnp.zeros((n, lanes), f32)
+    def own_sum(values, rows):
+        zc = lane(rows) % per
+        out = jnp.zeros((rows, lanes), f32)
         for first in sorted({0, W % fine, (W + lanes) % fine}):
             last = min([e for e in (W % fine, (W + lanes) % fine, fine) if e > first])
             part = values[first]
@@ -213,15 +214,21 @@
             out = out + jnp.where((zw >= W) & (zw < W + lanes), part, 0.0)
         return out
 
-    def send_totals(s, sums):
-        both = jnp.concatenate([split(tt0[h] + 0.2 * sums[h]) for h in range(HALVES)], axis=0)
-        tot = jnp.dot(both, wts[2 * lanes:4 * lanes], preferred_element_type=f32)
+    def send_totals(s, along_x):
+        parts = [(0, 8), (n - 8, 8)] if along_x else [(0, n)]
+        sums = []
+        for h in range(HALVES):
+            for row, rows in parts:
+                conc = own_sum([cc[s, h, z, pl.ds(mid + row, rows), :] for z in range(fine)], rows)
+                sums.append(split(tt0[h, row:row + rows] + 0.2 * conc))
+        tot = jnp.dot(jnp.concatenate(sums, axis=0), wts[2 * lanes:4 * lanes], preferred_element_type=f32)
         slot = lane(8) % per
         out = jnp.zeros((8, lanes), f32)
-        for i in range(HALVES * blocks):
-            out = jnp.where(slot == i, tot[8 * i:8 * i + 8], out)
-        ts[s] = out
-        start(total_copies(s))
+        places = [h * blocks + j for h in range(HALVES) for row, rows in parts for j in range(row // 8, (row + rows) // 8)]
+        for i, place in enumerate(places):
+            out = jnp.where(slot == place, tot[8 * i:8 * i + 8], out)
+        (td if along_x else ts)[s] = out
+        start(total_copies(s, along_x))
 
     def edge(h, rows):
         return lane(rows) < per if h == 0 else lane(rows) >= lanes - per
@@ -234,11 +241,10 @@
                 cr[h, z] = jnp.where(edge(h, n), 0.0, pltpu.roll(cc[s, 1 - h, z, center, :], shift[h], 1))
 
     for h in range(HALVES):
-        tt0[h] = own_sum([1.0 - 0.3 * stat[TEMP, h, z, center, :] for z in range(fine)])
-    send_totals(0, [own_sum([cc[0, h, z, center, :] for z in range(fine)]) for h in range(HALVES)])
+        tt0[h] = own_sum([1.0 - 0.3 * stat[TEMP, h, z, center, :] for z in range(fine)], n)
+    send_totals(0, True)
+    send_totals(0, False)
     turn(0)
-
-    zc_w = lane(wide) % per
 
     def insert(dst, packed, row, rows):
         zc, at_rows = lane(rows) % per, pl.ds(LO + row, rows)
@@ -258,12 +264,6 @@
             insert(dst, hz[b], b * (n + W), W)
 
     k_n, k_e = lane(n) % (2 * W), lane(W) % (2 * W)
-
-    arrive(static_copies(False))
-    for f in range(FIELDS):
-        insert(cells(f), jnp.where(k_n < W, szr[0, f], szr[1, f]), W, n)
-
-    up_rows, down_rows = pl.ds(LO + 1, wide), pl.ds(LO - 1, wide)
 
     def coefficients(row, rows):
         here, up, down, flat = pl.ds(LO + row, rows), pl.ds(LO + row + 1, rows), pl.ds(LO + row - 1, rows), pl.ds(row, rows)
@@ -297,91 +297,84 @@
                 tt[h, z, flat] = jnp.where(real, 1.0 - 0.3 * t, 0.0)
                 gr[h, z, flat] = jnp.where(real, gravity, 0.0)
 
-    zc_n = lane(n) % per
-    for h in range(HALVES):
-        for z in range(fine):
-            zw = fine * zc_n + z
-            rl[h, z] = jnp.where((zw >= W) & (zw < W + lanes), SOLUTE_RATE / (stat[LIQ, h, z, center, :] + 0.1), 0.0)
-    coefficients(8, wide - 16)
-    sent(static_copies(False))
-    arrive(static_copies(True))
-    for f in range(FIELDS):
-        insert_strips(cells(f), lambda b, h, z, f=f: sxr[b, f, h, z], lambda b, side, f=f: ser[b, side, f])
-    for row in (0, wide - 8):
-        coefficients(row, 8)
-    sent(static_copies(True))
-
-    def keep(p, r, h, z, v):
-        p[h, z + 1, window, :] = v
-        r[1 - h, z] = pltpu.roll(v, shift[1 - h], 1)
+    def keep(sweep, h, z, row, rows, v):
+        p, r = press[sweep], turned[sweep]
+        at_rows = pl.ds(LO + row, rows)
+        p[h, z + 1, at_rows, :] = v
+        r[1 - h, z, pl.ds(row, rows), :] = pltpu.roll(v, shift[1 - h], 1)
         if z == 0:
-            p[h, fine + 1, window, :] = pltpu.roll(v, lanes - 1, 1)
+            p[h, fine + 1, at_rows, :] = pltpu.roll(v, lanes - 1, 1)
         if z == fine - 1:
-            p[h, 0, window, :] = pltpu.roll(v, 1, 1)
+            p[h, 0, at_rows, :] = pltpu.roll(v, 1, 1)
 
     order = [0, fine - 1] + list(range(1, fine - 1))
 
     def carried(flow, own, other):
         return flow * jnp.where(flow > 0.0, own, other)
 
-    def step(s, final):
-        if s > 0:
-            sent(halo_copies(s, True))
-            sent(halo_copies(s, False))
-            sent(total_copies(s))
-            arrive(halo_copies(s, False))
-            insert(cc.at[s], jnp.where(k_n < W, zr[s, 0], zr[s, 1]), W, n)
-            arrive(halo_copies(s, True))
-            insert_strips(cc.at[s], lambda b, h, z: xr[s, b, h, z], lambda b, side: er[s, b, side])
-        sums = []
-        for h in range(HALVES):
-            for z in range(fine):
-                rh[h, z] = tt[h, z] + 0.2 * cc[s, h, z, window, :]
-            before = rh[h, 0]
+    def forces(s, row, rows):
+        here, flat = pl.ds(LO + row, rows), pl.ds(row, rows)
+        first_lane = lane(rows) % per == 0
+        for h in range(HALVES):
+            for z in range(fine):
+                rh[h, z, flat, :] = tt[h, z, flat, :] + 0.2 * cc[s, h, z, here, :]
+            before = rh[h, 0, flat, :]
             for z in range(1, W):
-                before = before + rh[h, z]
-            run = jnp.where(zc_w == 0, -before, 0.0)
-            for z in range(fine):
-                rho = rh[h, z]
-                pa[h, z + 1, window, :] = run + 0.5 * rho
+                before = before + rh[h, z, flat, :]
+            run = jnp.where(first_lane, -before, 0.0)
+            lo = half * (pltpu.roll(rh[h, fine - 1, flat, :], 1, 1) + rh[h, 0, flat, :])
+            lift[h, 0, here, :] = lo
+            for z in range(fine):
+                rho = rh[h, z, flat, :]
+                press[0][h, z + 1, here, :] = run + 0.5 * rho
                 run = run + rho
-            sums.append(run)
-            lo = half * (pltpu.roll(rh[h, fine - 1], 1, 1) + rh[h, 0])
-            lift[h, 0, window, :] = lo
-            for z in range(fine):
-                other = rh[h, z + 1] if z < fine - 1 else pltpu.roll(rh[h, 0], lanes - 1, 1)
-                hi = half * (rh[h, z] + other)
-                lift[h, z + 1, window, :] = hi
-                bb[h, z] = srcn[h, z] - azp[h, z] * hi + azm[h, z] * lo
+                other = rh[h, z + 1, flat, :] if z < fine - 1 else pltpu.roll(rh[h, 0, flat, :], lanes - 1, 1)
+                hi = half * (rho + other)
+                lift[h, z + 1, here, :] = hi
+                bb[h, z, flat, :] = srcn[h, z, flat, :] - azp[h, z, flat, :] * hi + azm[h, z, flat, :] * lo
                 lo = hi
-        if s == 0:
-            sent(total_copies(0))
-        arrive(total_copies(s))
-        total = [tr[s, side, 0] for side in range(3)]
-        for d in range(1, nz - 1):
-            total = [total[side] + tr[s, side, d] for side in range(3)]
-        slot = lane(8) % per
-        for h in range(HALVES):
-            off[h, 0:W] = jnp.where(slot == h * blocks + blocks - 1, total[0], 0.0)[8 - W:8]
-            for j in range(blocks):
-                off[h, W + 8 * j:W + 8 * j + 8] = jnp.where(slot == h * blocks + j, total[1], 0.0)
-            off[h, W + n:wide] = jnp.where(slot == h * blocks, total[2], 0.0)[0:W]
-        both = jnp.concatenate([jnp.concatenate([split(sums[h]), split(off[h])], axis=1) for h in range(HALVES)], axis=0)
-        above = jnp.dot(both, wts[...], preferred_element_type=f32)
+            sm[h, flat, :] = run
+
+    def above(parts):
+        rows_in = [(h, pl.ds(row, rows)) for h in range(HALVES) for row, rows in parts]
+        both = jnp.concatenate([jnp.concatenate([split(sm[h, at, :]), split(off[h, at, :])], axis=1) for h, at in rows_in], axis=0)
+        base = jnp.dot(both, wts[...], preferred_element_type=f32)
+        done = 0
+        for h in range(HALVES):
+            for row, rows in parts:
+                ab[h, pl.ds(row, rows), :] = base[done:done + rows]
+                done += rows
+
+    def heads(row, rows):
+        here, flat = pl.ds(LO + row, rows), pl.ds(row, rows)
         for z in order:
             for h in range(HALVES):
-                keep(pa, ra, h, z, gr[h, z] * (pa[h, z + 1, window, :] + above[h * wide:(h + 1) * wide]))
-
-        old, new, rold, rnew = pa, pb, ra, rb
-        for sweep in range(SWEEPS):
-            for z in order:
-                for h in range(HALVES):
-                    v = bb[h, z] + axp[h, z] * old[h, z + 1, up_rows, :] + axm[h, z] * old[h, z + 1, down_rows, :]
-                    v = v + (ays[h, z] * old[1 - h, z + 1, window, :] + ayr[h, z] * rold[h, z])
-                    v = v + (azp[h, z] * old[h, z + 2, window, :] + azm[h, z] * old[h, z, window, :])
-                    keep(new, rnew, h, z, v)
-            old, new, rold, rnew = new, old, rnew, rold
-
+                keep(0, h, z, row, rows, gr[h, z, flat, :] * (press[0][h, z + 1, here, :] + ab[h, flat, :]))
+
+    def relax(sweep, row, rows):
+        old, rold = press[sweep], turned[sweep]
+        here, flat = pl.ds(LO + row, rows), pl.ds(row, rows)
+        up, down = pl.ds(LO + row + 1, rows), pl.ds(LO + row - 1, rows)
+        for z in order:
+            for h in range(HALVES):
+                v = bb[h, z, flat, :] + axp[h, z, flat, :] * old[h, z + 1, up, :] + axm[h, z, flat, :] * old[h, z + 1, down, :]
+                v = v + (ays[h, z, flat, :] * old[1 - h, z + 1, here, :] + ayr[h, z, flat, :] * rold[h, z, flat, :])
+                v = v + (azp[h, z, flat, :] * old[h, z + 2, here, :] + azm[h, z, flat, :] * old[h, z, here, :])
+                keep(sweep + 1, h, z, row, rows, v)
+
+    def ends(row):
+        return [(row, 8), (wide - 8 - row, 8)]
+
+    def received(s, side):
+        total = tr[s, side, 0]
+        for d in range(1, nz - 1):
+            total = total + tr[s, side, d]
+        return total
+
+    old, rold = press[SWEEPS], turned[SWEEPS]
+
+    def step(s, final):
+        lead = W if s > 0 else 8
         def transport(row, rows):
             here, up, down = pl.ds(mid + row, rows), pl.ds(mid + row + 1, rows), pl.ds(mid + row - 1, rows)
             flat, inner = pl.ds(row, rows), pl.ds(W + row, rows)
@@ -427,18 +420,77 @@
             if row + rows == n:
                 es[s + 1, 1] = slab[rows - W:rows]
 
+        slot = lane(8) % per
+        if s > 0:
+            sent(halo_copies(s, True))
+            sent(halo_copies(s, False))
+            sent(total_copies(s, True))
+            sent(total_copies(s, False))
+            arrive(halo_copies(s, False))
+            insert(cc.at[s], jnp.where(k_n < W, zr[s, 0], zr[s, 1]), W, n)
+        else:
+            arrive(static_copies(False))
+            for f in range(FIELDS):
+                insert(cells(f), jnp.where(k_n < W, szr[0, f], szr[1, f]), W, n)
+            zc_n = lane(n) % per
+            for h in range(HALVES):
+                for z in range(fine):
+                    zw = fine * zc_n + z
+                    rl[h, z] = jnp.where((zw >= W) & (zw < W + lanes),
+                                         SOLUTE_RATE / (stat[LIQ, h, z, center, :] + 0.1), 0.0)
+            coefficients(lead, wide - 2 * lead)
+            sent(static_copies(False))
+            sent(total_copies(0, True))
+            sent(total_copies(0, False))
+        inner = (lead, wide - 2 * lead)
+        forces(s, *inner)
+        arrive(total_copies(s, False))
+        below = received(s, 1)
+        for h in range(HALVES):
+            for j in range(blocks):
+                off[h, W + 8 * j:W + 8 * j + 8] = jnp.where(slot == h * blocks + j, below, 0.0)
+        above([inner])
+        heads(*inner)
+        for sweep in range(SWEEPS):
+            relax(sweep, lead + 1 + sweep, wide - 2 * (lead + 1 + sweep))
+        transport(lead, n - 2 * lead)
+
+        if s > 0:
+            arrive(halo_copies(s, True))
+            insert_strips(cc.at[s], lambda b, h, z: xr[s, b, h, z], lambda b, side: er[s, b, side])
+        else:
+            arrive(static_copies(True))
+            for f in range(FIELDS):
+                insert_strips(cells(f), lambda b, h, z, f=f: sxr[b, f, h, z], lambda b, side, f=f: ser[b, side, f])
+            for end in ends(0):
+                coefficients(*end)
+            sent(static_copies(True))
+        for end in ends(0):
+            forces(s, *end)
+        arrive(total_copies(s, True))
+        left, right = received(s, 0), received(s, 2)
+        for h in range(HALVES):
+            off[h, 0:W] = jnp.where(slot == h * blocks + blocks - 1, left, 0.0)[8 - W:8]
+            off[h, W + n:wide] = jnp.where(slot == h * blocks, right, 0.0)[0:W]
+        above(ends(0))
+        for end in ends(0):
+            heads(*end)
+        for sweep in range(SWEEPS):
+            for end in ends(sweep + 1):
+                relax(sweep, *end)
         if not final:
             transport(0, 8)
             transport(n - 8, 8)
             start(halo_copies(s + 1, True))
-            transport(8, n - 16)
+            send_totals(s + 1, True)
             start(halo_copies(s + 1, False))
-            send_totals(s + 1, [own_sum([cc[s + 1, h, z, center, :] for z in range(fine)]) for h in range(HALVES)])
+            send_totals(s + 1, False)
             turn(s + 1)
         else:
             out = pltpu.make_async_copy(old.at[:, pl.ds(1, fine), center, :], p_out, out_sem.at[0])
             out.start()
-            transport(0, n)
+            transport(0, 8)
+            transport(n - 8, 8)
             last = pltpu.make_async_copy(cc.at[s + 1, :, :, center, :], c_out, out_sem.at[1])
             last.start()
             out.wait()
@@ -500,20 +552,20 @@
     slots = (HALVES, fine + 2, rows, lanes)
     scratch = [pltpu.VMEM((ny, n, lanes), a.dtype) for a in args]
     scratch += [vmem(ny, n, lanes)] * 2 + [vmem(FIELDS, ny, 2 * W, lanes)]
-    scratch += [vmem(FIELDS - 1, *padded), vmem(STEPS + 1, *padded), vmem(*slots), vmem(*slots)]
-    scratch += [vmem(*plain), vmem(*plain), vmem(*own)]
+    scratch += [vmem(FIELDS - 1, *padded), vmem(STEPS + 1, *padded), vmem(*own)]
+    scratch += [vmem(*slots)] * W + [vmem(*plain)] * W
     scratch += [vmem(*plain)] * 10
     scratch += [vmem(*padded), vmem(fine, rows, lanes), vmem(*padded), vmem(HALVES, fine + 1, rows, lanes),
                 vmem(HALVES, fine + 1, rows, lanes), vmem(*own), vmem(*plain)]
-    scratch += [pltpu.VMEM((4 * lanes, lanes), jnp.bfloat16), vmem(2, W, lanes), vmem(HALVES, wide, lanes),
-                vmem(HALVES, n, lanes)]
+    scratch += [pltpu.VMEM((4 * lanes, lanes), jnp.bfloat16), vmem(2, W, lanes)] + [vmem(HALVES, wide, lanes)] * 3
+    scratch += [vmem(HALVES, n, lanes)]
     scratch += [vmem(STEPS, 2, HALVES, fine, W, lanes)] * 2
     scratch += [vmem(STEPS, n, lanes), vmem(STEPS, 2, n, lanes)]
     scratch += [vmem(STEPS, 2, W, lanes), vmem(STEPS, 2, 2, W, lanes)]
-    scratch += [vmem(STEPS, 8, lanes), vmem(STEPS, 3, nz - 1, 8, lanes)]
+    scratch += [vmem(STEPS, 8, lanes)] * 2 + [vmem(STEPS, 3, nz - 1, 8, lanes)]
     scratch += [vmem(2, FIELDS, HALVES, fine, W, lanes)] * 2
     scratch += [vmem(FIELDS, n, lanes), vmem(2, FIELDS, n, lanes), vmem(2, FIELDS, W, lanes), vmem(2, 2, FIELDS, W, lanes)]
-    scratch += [pltpu.SemaphoreType.DMA((STEPS, copies))] * 2 + [pltpu.SemaphoreType.DMA((8,))] * 2
+    scratch += [pltpu.SemaphoreType.DMA((copies,)), pltpu.SemaphoreType.DMA((STEPS, copies))] + [pltpu.SemaphoreType.DMA((8,))] * 2
     scratch += [pltpu.SemaphoreType.DMA((5,)), pltpu.SemaphoreType.DMA((2,))]
     cells = pl.pallas_call(
         functools.partial(kernel, nx, nz),

time: 37.2 us -> 35.8 us (0.962); the launches traced: 36.4 us -> 35.5 us
  Pallas kernels: 35.8 us -> 34.7 us
    pallas_call x1, Pallas kernels: 33.2 us -> 32.1 us  [on_device(): pl.pallas_call(functools.partial(kernel, nx, nz), out_shape=[jax.ShapeDty...]
where the time goes in v3:
time: 35.8 us; the launch traced here: 35.5 us
  Pallas kernels  34.7 us (97%)
  between operations  0.8 us (2%)
    pallas_call x1, Pallas kernels, on_device(): pl.pallas_call(functools.partial(kernel, nx, nz), out_shape=[jax.ShapeDty...  32.1 us
    pallas_call x1, Pallas kernels, on_device(): pl.pallas_call(hand_out, out_shape=[jax.ShapeDtypeStruct((ny, n, lanes),...  2.62 us

profile of v3, /device:TPU:9, one launch (start us, length us, event | category | flops | bytes accessed | tf_op | source)
XLA Modules:
  0.0 35.5 jit_solution(18315393887809110788)
XLA Ops:
  0.6 32.1 %shard_map.68 = (f32[2,9,48,128]{3,2,1,0:T(8,128)}, f32[2,9,48,128]{3,2,1,0:T(8,128)}) custom-call(f32[16,48,128]{2,1,0:T(8,128)} %refs_0_.1, f32[16,48,128]{2,1,0:T(8,128)} %refs_1_.1, f32[16,48,128]{2,1,0:T(8,128)} %refs_2_.1, f32[16,48,128]{2,1,0:T(8,128)} %refs_3_.1, s32[16,48,128]{2,1,0:T(8,128)} %refs_4_.1), custom_call_target="tpu_custom_call" | custom-call | tf_op jit(solution)/shard_map/pallas_call | solution.py:570
  32.7 2.6 %shard_map.69 = (f32[16,48,128]{2,1,0:T(8,128)}, f32[16,48,128]{2,1,0:T(8,128)}) custom-call(f32[2,9,48,128]{3,2,1,0:T(8,128)} %get-tuple-element.4.p, f32[2,9,48,128]{3,2,1,0:T(8,128)} %get-tuple-element.5.c), custom_call_target="tpu_custom_call" | custom-call | tf_op jit(solution)/shard_map/pallas_call | solution.py:579

commit v4 on v3

--- a/solution.py
+++ b/solution.py
@@ -80,20 +80,26 @@
                        send_sem.at[len(near) + m], recv_sem.at[s, len(near) + m], dx, dz)
                 for m, (dx, dz) in enumerate(below) if (dx != 0) == along_x]
 
-    def static_copies(along_x):
+    def static_copies(dz_only):
         out = []
         for m, (dx, dz) in enumerate(near):
             a, b = (1, 0) if dx > 0 else (0, 1)
             side = 0 if dz > 0 else 1
-            if dz == 0:
-                src, dst = sxs.at[a], sxr.at[b]
-            elif dx == 0:
+            if dx == 0:
                 src, dst = szs, szr.at[side]
+            elif dz != 0:
+                src, dst = ses.at[a], ser.at[b, side]
             else:
-                src, dst = ses.at[a], ser.at[b, side]
-            if (dx != 0) == along_x:
+                continue
+            if (dx == 0) == dz_only:
                 out.append(remote(src, dst, st_send.at[m], st_recv.at[m], dx, dz))
-        return sorted(out, key=lambda item: item[1] != 0)
+        return out
+
+    def static_strips(fields, base):
+        return [remote(sxs.at[a, fields], sxr.at[1 - a, fields], st_send.at[base + a], st_recv.at[base + a], dx, 0)
+                for a, dx in ((1, 1), (0, -1))]
+
+    still, moving = pl.ds(0, FIELDS - 1), pl.ds(FIELDS - 1, 1)
 
     def start(copies):
         for dx, dz, c in copies:
@@ -190,8 +196,10 @@
             sxs[1, f, h, z] = v[W:2 * W]
         spread(lambda y, f=f: strip[f, y], put, 2 * W)
     pl.semaphore_wait(barrier, count)
+    start(static_strips(still, 8))
+    start(static_copies(False))
     start(static_copies(True))
-    start(static_copies(False))
+    start(static_strips(moving, 10))
 
     def cells(f):
         return cc.at[0] if f == CONC else stat.at[f]
@@ -422,14 +430,10 @@
 
         slot = lane(8) % per
         if s > 0:
-            sent(halo_copies(s, True))
-            sent(halo_copies(s, False))
-            sent(total_copies(s, True))
-            sent(total_copies(s, False))
             arrive(halo_copies(s, False))
             insert(cc.at[s], jnp.where(k_n < W, zr[s, 0], zr[s, 1]), W, n)
         else:
-            arrive(static_copies(False))
+            arrive(static_copies(True))
             for f in range(FIELDS):
                 insert(cells(f), jnp.where(k_n < W, szr[0, f], szr[1, f]), W, n)
             zc_n = lane(n) % per
@@ -439,9 +443,6 @@
                     rl[h, z] = jnp.where((zw >= W) & (zw < W + lanes),
                                          SOLUTE_RATE / (stat[LIQ, h, z, center, :] + 0.1), 0.0)
             coefficients(lead, wide - 2 * lead)
-            sent(static_copies(False))
-            sent(total_copies(0, True))
-            sent(total_copies(0, False))
         inner = (lead, wide - 2 * lead)
         forces(s, *inner)
         arrive(total_copies(s, False))
@@ -455,16 +456,32 @@
             relax(sweep, lead + 1 + sweep, wide - 2 * (lead + 1 + sweep))
         transport(lead, n - 2 * lead)
 
+        def outs(part, row, rows):
+            at, to = pl.ds(mid + row, rows), pl.ds(row, rows)
+            return [pltpu.make_async_copy(old.at[:, pl.ds(1, fine), at, :], p_out.at[:, :, to, :], out_sem.at[2 * part]),
+                    pltpu.make_async_copy(cc.at[s + 1, :, :, at, :], c_out.at[:, :, to, :], out_sem.at[2 * part + 1])]
+
+        if final:
+            leaving = outs(0, 8, n - 16)
+            for out in leaving:
+                out.start()
+
         if s > 0:
             arrive(halo_copies(s, True))
             insert_strips(cc.at[s], lambda b, h, z: xr[s, b, h, z], lambda b, side: er[s, b, side])
         else:
-            arrive(static_copies(True))
-            for f in range(FIELDS):
-                insert_strips(cells(f), lambda b, h, z, f=f: sxr[b, f, h, z], lambda b, side, f=f: ser[b, side, f])
+            arrive(static_strips(still, 8))
+            arrive(static_copies(False))
+
+            def place(f):
+                insert_strips(cells(f), lambda b, h, z: sxr[b, f, h, z], lambda b, side: ser[b, side, f])
+
+            for f in (PERM, TEMP, LIQ):
+                place(f)
             for end in ends(0):
                 coefficients(*end)
-            sent(static_copies(True))
+            arrive(static_strips(moving, 10))
+            place(CONC)
         for end in ends(0):
             forces(s, *end)
         arrive(total_copies(s, True))
@@ -478,23 +495,32 @@
         for sweep in range(SWEEPS):
             for end in ends(sweep + 1):
                 relax(sweep, *end)
+        if s > 0:
+            sent(halo_copies(s, True))
+            sent(halo_copies(s, False))
+        else:
+            sent(static_strips(still, 8))
+            sent(static_strips(moving, 10))
+            sent(static_copies(True))
+            sent(static_copies(False))
+        sent(total_copies(s, True))
+        sent(total_copies(s, False))
         if not final:
             transport(0, 8)
             transport(n - 8, 8)
+            send_totals(s + 1, False)
+            start(halo_copies(s + 1, False))
             start(halo_copies(s + 1, True))
             send_totals(s + 1, True)
-            start(halo_copies(s + 1, False))
-            send_totals(s + 1, False)
             turn(s + 1)
         else:
-            out = pltpu.make_async_copy(old.at[:, pl.ds(1, fine), center, :], p_out, out_sem.at[0])
-            out.start()
             transport(0, 8)
             transport(n - 8, 8)
-            last = pltpu.make_async_copy(cc.at[s + 1, :, :, center, :], c_out, out_sem.at[1])
-            last.start()
-            out.wait()
-            last.wait()
+            rest = outs(1, 0, 8) + outs(2, n - 8, 8)
+            for out in rest:
+                out.start()
+            for out in leaving + rest:
+                out.wait()
 
     for s in range(STEPS):
         step(s, s == STEPS - 1)
@@ -565,8 +591,8 @@
     scratch += [vmem(STEPS, 8, lanes)] * 2 + [vmem(STEPS, 3, nz - 1, 8, lanes)]
     scratch += [vmem(2, FIELDS, HALVES, fine, W, lanes)] * 2
     scratch += [vmem(FIELDS, n, lanes), vmem(2, FIELDS, n, lanes), vmem(2, FIELDS, W, lanes), vmem(2, 2, FIELDS, W, lanes)]
-    scratch += [pltpu.SemaphoreType.DMA((copies,)), pltpu.SemaphoreType.DMA((STEPS, copies))] + [pltpu.SemaphoreType.DMA((8,))] * 2
-    scratch += [pltpu.SemaphoreType.DMA((5,)), pltpu.SemaphoreType.DMA((2,))]
+    scratch += [pltpu.SemaphoreType.DMA((copies,)), pltpu.SemaphoreType.DMA((STEPS, copies))] + [pltpu.SemaphoreType.DMA((12,))] * 2
+    scratch += [pltpu.SemaphoreType.DMA((5,)), pltpu.SemaphoreType.DMA((6,))]
     cells = pl.pallas_call(
         functools.partial(kernel, nx, nz),
         out_shape=[jax.ShapeDtypeStruct(own, jnp.float32)] * 2,

time: 35.8 us -> 35.7 us (level)
  no operation moved by 1% of the time
where the time goes in v4:
time: 35.7 us; the launch traced here: 35.6 us
  Pallas kernels  34.8 us (97%)
  between operations  0.8 us (2%)
    pallas_call x1, Pallas kernels, on_device(): pl.pallas_call(functools.partial(kernel, nx, nz), out_shape=[jax.ShapeDty...  32.1 us
    pallas_call x1, Pallas kernels, on_device(): pl.pallas_call(hand_out, out_shape=[jax.ShapeDtypeStruct((ny, n, lanes),...  2.62 us

profile of v4, /device:TPU:9, one launch (start us, length us, event | category | flops | bytes accessed | tf_op | source)
XLA Modules:
  0.0 35.6 jit_solution(15239070574215323154)
XLA Ops:
  0.6 32.1 %shard_map.68 = (f32[2,9,48,128]{3,2,1,0:T(8,128)}, f32[2,9,48,128]{3,2,1,0:T(8,128)}) custom-call(f32[16,48,128]{2,1,0:T(8,128)} %refs_0_.1, f32[16,48,128]{2,1,0:T(8,128)} %refs_1_.1, f32[16,48,128]{2,1,0:T(8,128)} %refs_2_.1, f32[16,48,128]{2,1,0:T(8,128)} %refs_3_.1, s32[16,48,128]{2,1,0:T(8,128)} %refs_4_.1), custom_call_target="tpu_custom_call" | custom-call | tf_op jit(solution)/shard_map/pallas_call | solution.py:596
  32.8 2.6 %shard_map.69 = (f32[16,48,128]{2,1,0:T(8,128)}, f32[16,48,128]{2,1,0:T(8,128)}) custom-call(f32[2,9,48,128]{3,2,1,0:T(8,128)} %get-tuple-element.4.p, f32[2,9,48,128]{3,2,1,0:T(8,128)} %get-tuple-element.5.c), custom_call_target="tpu_custom_call" | custom-call | tf_op jit(solution)/shard_map/pallas_call | solution.py:605
